TPU v7x, 128 devices: a whole 4x4x4 slice. The times are simulated.
128 devices in a mesh: shard: 2 (over x_hi), ctx: 16 (over x_lo, z, core), tp: 4 (over y).
Axes of the slice: x: 4 (x_hi: 2, x_lo: 2; x = x_hi * 2 + x_lo), y: 4, z: 4, core: 2. Of those that a mesh axis runs over, the one named last changes fastest.
Arguments:
- block_input: bfloat16 [4, 4096, 1024], P('shard', 'ctx', 'tp'), may hold values from -6 to 6
- in_proj: bfloat16 [1024, 3, 1024], P('shard', None, 'tp'), may hold values from -0.1875 to 0.1875
- out_proj: bfloat16 [1024, 1024], P('tp', 'shard'), may hold values from -0.1875 to 0.1875
- gate_proj: bfloat16 [1024, 4608], P('shard', 'tp'), may hold values from -0.1875 to 0.1875
- up_proj: bfloat16 [1024, 4608], P('shard', 'tp'), may hold values from -0.1875 to 0.1875
- down_proj: bfloat16 [4608, 1024], P('tp', 'shard'), may hold values from -0.09375 to 0.09375
- mixer_gain: float32 [1024], P('tp'), may hold values from 0.5 to 1.5
- ffn_gain: float32 [1024], P('tp'), may hold values from 0.5 to 1.5
- conv_kernel: float32 [3, 1024], P(None, 'tp'), may hold values from -3.5 to 3.5
- cotangent: bfloat16 [4, 4096, 1024], P('shard', 'ctx', 'tp'), may hold values from -6 to 6
Outputs:
- block_out: bfloat16 [4, 4096, 1024], P('shard', 'ctx', 'tp')
- input_grad: float32 [4, 4096, 1024], P('shard', 'ctx', 'tp')
- in_proj_grad: float32 [1024, 3, 1024], P(('shard', 'ctx'), None, 'tp')
- out_proj_grad: float32 [1024, 1024], P('tp', ('shard', 'ctx'))
- gate_grad: float32 [1024, 4608], P(('shard', 'ctx'), 'tp')
- up_grad: float32 [1024, 4608], P(('shard', 'ctx'), 'tp')
- down_grad: float32 [4608, 1024], P('tp', ('shard', 'ctx'))
- mixer_gain_grad: float32 [1024], P('tp')
- ffn_gain_grad: float32 [1024], P('tp')
- kernel_grad: float32 [3, 1024], P(None, 'tp')
All inputs are finite; a program needn't handle non-finite values.
Results may differ from a plain program's by a relative error of at most 0.0088.
Values may be sent and summed in bfloat16 or wider, within the bound.
A program may use at most 128 MiB of HBM per device.

v0:
```python
import jax
import jax.numpy as jnp
from jax import lax
from jax.sharding import PartitionSpec as P

EPS = 1e-05


def from_everyone(x, axis):
    count = lax.axis_size(axis)
    return lax.all_to_all(jnp.broadcast_to(x[None], (count, *x.shape)), axis, 0, 0, tiled=True)


def taken_together(x, axis):
    return from_everyone(x, axis).sum(axis=0)


def joined_along(tiles, dim):
    tiles = jnp.moveaxis(tiles, 0, dim)
    lengths = tiles.shape
    return tiles.reshape(*lengths[:dim], lengths[dim] * lengths[dim + 1], *lengths[dim + 2 :])


def gather_directly(x, axis, dim):
    tiles = from_everyone(x, axis)
    return joined_along(tiles, dim)


def in_blocks(x, dim, count):
    before, after = (x.shape[:dim], x.shape[dim + 1 :])
    return jnp.moveaxis(x.reshape(*before, count, -1, *after), dim, 0)


def sent_and_summed(x, axis, dim):
    tiles = in_blocks(x, dim, lax.axis_size(axis))
    arrived = lax.all_to_all(tiles, axis, split_axis=0, concat_axis=0, tiled=True)
    return arrived.sum(axis=0)


def from_behind(block, axis, distance):
    devices = range(lax.axis_size(axis))
    route = [(i - distance, i) for i in devices if i - distance in devices]
    return lax.ppermute(block, axis, route)


def sent_together(arrays, axis, dim, along):
    widths = [a.shape[along] for a in arrays]
    both = jnp.concatenate(arrays, axis=along)
    whole = lax.psum_scatter(both, axis, scatter_dimension=dim, tiled=True)
    return tuple(jnp.split(whole, [sum(widths[:k]) for k in range(1, len(widths))], axis=along))


def together(arrays, axis):
    ends = [0]
    for a in arrays:
        ends.append(ends[-1] + a.size)
    total = taken_together(jnp.concatenate([a.ravel() for a in arrays]), axis)
    return tuple((total[b:e].reshape(a.shape) for a, b, e in zip(arrays, ends, ends[1:])))


def row_total(values):
    return taken_together(jnp.sum(values, axis=-1), "tp")


def gather_features(values):
    return gather_directly(values, "tp", 2)


def sum_partials(values):
    return sent_and_summed(values, "tp", 2)


def row_scale(values, full_width):
    return lax.rsqrt(row_total(values * values) / full_width + EPS)[..., None]


def norm_back(grad_in, values, scale_rows, norm_gain, full_width):
    weighted = grad_in * norm_gain
    inner_sum = row_total(weighted * values)[..., None]
    grad_values = scale_rows * weighted - values * scale_rows**3 * inner_sum / full_width
    grad_gain = jnp.sum(grad_in * values * scale_rows, axis=(0, 1))
    return (grad_values, grad_gain)


def on_device(
    block_input,
    in_proj,
    out_proj,
    gate_proj,
    up_proj,
    down_proj,
    mixer_gain,
    ffn_gain,
    conv_kernel,
    cotangent,
):
    single_float = jnp.float32
    bf16 = jnp.bfloat16
    full_width = block_input.shape[-1] * lax.axis_size("tp")
    inputs = block_input.astype(single_float)
    input_weight, output_weight, gate_weight, up_weight, down_weight = (
        lax.all_gather(in_proj, "shard", axis=0, tiled=True),
        lax.all_gather(out_proj, "shard", axis=1, tiled=True),
        lax.all_gather(gate_proj, "shard", axis=0, tiled=True),
        lax.all_gather(up_proj, "shard", axis=0, tiled=True),
        lax.all_gather(down_proj, "shard", axis=1, tiled=True),
    )
    scale_one = row_scale(inputs, full_width)
    first_normalized = gather_features((inputs * scale_one * mixer_gain).astype(bf16))
    projected_rows = jnp.einsum(
        "iqa,ayj->iqyj", first_normalized, input_weight, preferred_element_type=single_float
    )
    b_gate = projected_rows[:, :, 0]
    c_gate = projected_rows[:, :, 1]
    x_in = projected_rows[:, :, 2]
    mixed = (b_gate * x_in).astype(bf16)
    length = mixed.shape[1]
    edge_rows = from_behind(mixed[:, length - 2 :], "ctx", 1)
    padded = jnp.concatenate([edge_rows, mixed], axis=1).astype(single_float)
    convolved = (
        conv_kernel[0] * padded[:, :length]
        + conv_kernel[1] * padded[:, 1 : length + 1]
        + conv_kernel[2] * padded[:, 2:]
    )
    gated_product = (c_gate * convolved).astype(bf16)
    branch_output = jnp.einsum(
        "ynz,zj->ynj", gated_product, output_weight, preferred_element_type=single_float
    )
    residual_state = inputs + sum_partials(branch_output)
    scale_two = row_scale(residual_state, full_width)
    second_normalized = gather_features((residual_state * scale_two * ffn_gain).astype(bf16))
    gate_activation = jnp.einsum(
        "zxw,wt->zxt", second_normalized, gate_weight, preferred_element_type=single_float
    )
    up_activation = jnp.einsum(
        "zxw,wt->zxt", second_normalized, up_weight, preferred_element_type=single_float
    )
    sigmoid_gate = jax.nn.sigmoid(gate_activation)
    activated = gate_activation * sigmoid_gate
    hidden_state = (activated * up_activation).astype(bf16)
    feedforward_output = jnp.einsum(
        "hcu,uv->hcv", hidden_state, down_weight, preferred_element_type=single_float
    )
    block_out = (residual_state + sum_partials(feedforward_output)).astype(bf16)
    full_cotangent_grad = gather_features(cotangent)
    hidden_gradient = jnp.einsum(
        "mxg,yg->mxy", full_cotangent_grad, down_weight, preferred_element_type=single_float
    )
    local_down_weight = jnp.einsum(
        "jzo,jzh->oh", hidden_state, full_cotangent_grad, preferred_element_type=single_float
    )
    gate_gradient = (
        hidden_gradient
        * up_activation
        * sigmoid_gate
        * (1.0 + gate_activation * (1.0 - sigmoid_gate))
    ).astype(bf16)
    up_gradient = (hidden_gradient * activated).astype(bf16)
    local_gate_weight = jnp.einsum(
        "joi,joq->iq", second_normalized, gate_gradient, preferred_element_type=single_float
    )
    local_up_weight = jnp.einsum(
        "joi,joq->iq", second_normalized, up_gradient, preferred_element_type=single_float
    )
    norm_part_gradient = jnp.einsum(
        "ypt,kt->ypk", gate_gradient, gate_weight, preferred_element_type=single_float
    )
    norm_part_gradient = norm_part_gradient + jnp.einsum(
        "ypt,kt->ypk", up_gradient, up_weight, preferred_element_type=single_float
    )
    d_norm_two = sum_partials(norm_part_gradient)
    d_resid_norm, ffn_gain_local = norm_back(
        d_norm_two, residual_state, scale_two, ffn_gain, full_width
    )
    d_resid = cotangent.astype(single_float) + d_resid_norm
    branch_gradient = gather_features(d_resid.astype(bf16))
    local_output_weight = jnp.einsum(
        "pmn,pmi->ni", gated_product, branch_gradient, preferred_element_type=single_float
    )
    gated_gradient = jnp.einsum(
        "bkg,ug->bku", branch_gradient, output_weight, preferred_element_type=single_float
    )
    d_conv = gated_gradient * c_gate
    d_cgate = gated_gradient * convolved
    conv_padded = jnp.pad(d_conv, ((0, 0), (2, 2), (0, 0)))
    d_mixed_pad = (
        conv_kernel[0] * conv_padded[:, 2:]
        + conv_kernel[1] * conv_padded[:, 1 : length + 3]
        + conv_kernel[2] * conv_padded[:, : length + 2]
    )
    returned = from_behind(d_mixed_pad[:, :2], "ctx", -1)
    d_mixed = d_mixed_pad[:, 2:] + jnp.pad(returned, ((0, 0), (length - 2, 0), (0, 0)))
    kernel_local = jnp.stack(
        [
            jnp.sum(d_conv * padded[:, :length], axis=(0, 1)),
            jnp.sum(d_conv * padded[:, 1 : length + 1], axis=(0, 1)),
            jnp.sum(d_conv * padded[:, 2:], axis=(0, 1)),
        ],
        axis=0,
    )
    projected_gradient = jnp.stack([d_mixed * x_in, d_cgate, d_mixed * b_gate], axis=2).astype(bf16)
    local_input_weight = jnp.einsum(
        "bqa,bqzp->azp", first_normalized, projected_gradient, preferred_element_type=single_float
    )
    d_norm_one = sum_partials(
        jnp.einsum(
            "vjyb,qyb->vjq", projected_gradient, input_weight, preferred_element_type=single_float
        )
    )
    d_input_norm, mixer_gain_local = norm_back(
        d_norm_one, inputs, scale_one, mixer_gain, full_width
    )
    input_grad = d_resid + d_input_norm
    in_proj_grad, out_proj_grad, gate_grad, up_grad, down_grad = (
        lax.psum_scatter(local_input_weight, ("shard", "ctx"), scatter_dimension=0, tiled=True),
        lax.psum_scatter(local_output_weight, ("shard", "ctx"), scatter_dimension=1, tiled=True),
        *sent_together((local_gate_weight, local_up_weight), ("shard", "ctx"), 0, 1),
        lax.psum_scatter(local_down_weight, ("shard", "ctx"), scatter_dimension=1, tiled=True),
    )
    mixer_gain_grad, ffn_gain_grad, kernel_grad = together(
        (mixer_gain_local, ffn_gain_local, kernel_local), ("shard", "ctx")
    )
    return (
        block_out,
        input_grad,
        in_proj_grad,
        out_proj_grad,
        gate_grad,
        up_grad,
        down_grad,
        mixer_gain_grad,
        ffn_gain_grad,
        kernel_grad,
    )


def solution(mesh):
    return jax.shard_map(
        on_device,
        mesh=mesh,
        in_specs=(
            P("shard", "ctx", "tp"),
            P("shard", None, "tp"),
            P("tp", "shard"),
            P("shard", "tp"),
            P("shard", "tp"),
            P("tp", "shard"),
            P("tp"),
            P("tp"),
            P(None, "tp"),
            P("shard", "ctx", "tp"),
        ),
        out_specs=(
            P("shard", "ctx", "tp"),
            P("shard", "ctx", "tp"),
            P(("shard", "ctx"), None, "tp"),
            P("tp", ("shard", "ctx")),
            P(("shard", "ctx"), "tp"),
            P(("shard", "ctx"), "tp"),
            P("tp", ("shard", "ctx")),
            P("tp"),
            P("tp"),
            P(None, "tp"),
        ),
        check_vma=False,
    )
```

profile of v0, /device:TPU:0, one launch (start us, length us, event | category | flops | bytes accessed | tf_op | source)
XLA Modules:
  0.0 540.6 jit_solution(1907885705509384484)
XLA Ops:
  8.9 9.7 %all_to_all.66 = f32[4,2,256]{2,1,0:T(2,128)S(1)} all-to-all(f32[4,2,256]{2,1,0:T(2,128)S(1)} %broadcast_in_dim.18), channel_id=1, replica_groups=mesh['shard'=2,'ctx'=16,'tp'=4] {'tp'}, dimensions={0} | all-to-all | bytes 16384 | tf_op jit(solution)/shard_map/all_to_all | solution.py:11
  19.8 3.5 all-to-all-start.1
  24.1 13.1 %all-to-all-done.1 = bf16[4,2,256,256]{3,2,1,0:T(8,128)(2,1)S(1)} async-done(((bf16[4,2,256,256]{3,2,1,0:T(8,128)(2,1)}), bf16[4,2,256,256]{3,2,1,0:T(8,128)(2,1)S(1)}, u32[]{:S(2)}, u32[]{:S(2)}) %all-to-all-start.1) | async-done | bytes 1048608 | tf_op jit(solution)/shard_map/all_to_all | solution.py:11
  38.8 4.6 all-gather.5.cloned.1.call-done
  43.4 2.4 fusion.15
  45.9 1.7 collective-permute-start
  47.6 10.5 %all_gather.16 = bf16[256,1024]{1,0:T(8,128)(2,1)S(1)} all-gather(bf16[256,512]{1,0:T(8,128)(2,1)S(1)} %copy-done.15), channel_id=1, replica_groups=mesh['shard'=2,'ctx'=16,'tp'=4] {'shard'}, dimensions={1}, use_global_device_ids=true | all-gather | bytes 786432 | tf_op jit(solution)/shard_map/all_gather | solution.py:103
  61.2 4.4 all-to-all-start.2
  66.2 26.9 %all-to-all-done.2 = f32[4,2,256,256]{3,2,1,0:T(8,128)} async-done(((f32[4,2,256,256]{3,2,1,0:T(8,128)}), f32[4,2,256,256]{3,2,1,0:T(8,128)}, u32[]{:S(2)}, u32[]{:S(2)}) %all-to-all-start.2) | async-done | bytes 2097184 | tf_op jit(solution)/shard_map/all_to_all | solution.py:36
  93.1 1.9 reduce_sum.164
  95.2 7.7 %all_to_all.67 = f32[4,2,256]{2,1,0:T(2,128)S(1)} all-to-all(f32[4,2,256]{2,1,0:T(2,128)S(1)} %broadcast_in_dim.20), channel_id=1, replica_groups=mesh['shard'=2,'ctx'=16,'tp'=4] {'tp'}, dimensions={0} | all-to-all | bytes 16384 | tf_op jit(solution)/shard_map/all_to_all | solution.py:11
  103.9 3.5 all-to-all-start.6
  108.3 13.6 %all-to-all-done.6 = bf16[4,2,256,256]{3,2,1,0:T(8,128)(2,1)S(1)} async-done(((bf16[4,2,256,256]{3,2,1,0:T(8,128)(2,1)}), bf16[4,2,256,256]{3,2,1,0:T(8,128)(2,1)S(1)}, u32[]{:S(2)}, u32[]{:S(2)}) %all-to-all-start.6) | async-done | bytes 1048608 | tf_op jit(solution)/shard_map/all_to_all | solution.py:11
  121.9 2.0 broadcast_in_dim.21
  123.9 4.3 all-to-all-start.4
  129.6 5.0 fusion
  134.5 7.4 %all-to-all-done.4 = bf16[4,2,256,256]{3,2,1,0:T(8,128)(2,1)} async-done(((bf16[4,2,256,256]{3,2,1,0:T(8,128)(2,1)}), bf16[4,2,256,256]{3,2,1,0:T(8,128)(2,1)}, u32[]{:S(2)}, u32[]{:S(2)}) %all-to-all-start.4) | async-done | bytes 1048608 | tf_op jit(solution)/shard_map/all_to_all | solution.py:11
  143.3 4.6 fusion.6
  147.9 19.1 %all-gather.7.cloned.1.call-done = bf16[1024,1152]{1,0:T(8,128)(2,1)} async-done(((bf16[512,1152]{1,0:T(8,128)(2,1)}), bf16[1024,1152]{1,0:T(8,128)(2,1)}) %all-gather.7.cloned.1.call-update) | async-done | bytes 2359312 | tf_op jit(solution)/shard_map/all_gather | solution.py:104
  167.0 6.5 %multiply_convert_fusion.1 = (bf16[2,256,1152]{2,1,0:T(8,128)(2,1)S(1)}, bf16[2,256,1152]{2,1,0:T(8,128)(2,1)S(1)}, bf16[2,256,1152]{2,1,0:T(8,128)(2,1)}) fusion(f32[2,256,1152]{2,1,0:T(8,128)} %fusion, f32[2,256,1152]{2,1,0:T(8,128)} %fusion.6, bf16[2,256,1024]{2,1,0:T(8,128)(2,1)S(1)} %bitcast.148, bf16[1024,1152]{1,0:T(8,128)(2,1)} %all-gather.7.cloned.1.call-done), kind=kOutput, calls=%fused_computation.17 | convolution fusion | flops 1216806912 | bytes 11665408 | tf_op jit(solution)/shard_map/zxw,wt->zxt/dot_general | solution.py:132
  173.5 1.6 convolution_bitcast_fusion.2
  175.1 3.8 convolution_bitcast_fusion.1
  178.9 6.7 %pad_maximum_fusion = f32[1024,2304]{1,0:T(8,128)} fusion(f32[1024,1152]{1,0:T(8,128)} %convolution_bitcast_fusion.1, f32[1024,1152]{1,0:T(8,128)S(1)} %convolution_bitcast_fusion.2), kind=kLoop, calls=%fused_computation | loop fusion | flops 2359296 | bytes 18874368 | tf_op jit(solution)/shard_map/concatenate | solution.py:48
  185.7 3.7 fusion.4
  189.4 1.6 fusion.17
  191.2 30.5 %all_to_all.68 = f32[4,2,256,256]{3,2,1,0:T(8,128)} all-to-all(f32[4,2,256,256]{3,2,1,0:T(8,128)S(1)} %bitcast.154), channel_id=1, replica_groups=mesh['shard'=2,'ctx'=16,'tp'=4] {'tp'}, dimensions={0} | all-to-all | bytes 4194304 | tf_op jit(solution)/shard_map/all_to_all | solution.py:36
  221.7 1.9 reduce_sum.168
  223.9 7.7 %all_to_all.69 = f32[4,2,256]{2,1,0:T(2,128)S(1)} all-to-all(f32[4,2,256]{2,1,0:T(2,128)S(1)} %broadcast_in_dim.23), channel_id=1, replica_groups=mesh['shard'=2,'ctx'=16,'tp'=4] {'tp'}, dimensions={0} | all-to-all | bytes 16384 | tf_op jit(solution)/shard_map/all_to_all | solution.py:11
  232.0 15.6 %all_to_all.70 = bf16[4,2,256,256]{3,2,1,0:T(8,128)(2,1)S(1)} all-to-all(bf16[4,2,256,256]{3,2,1,0:T(8,128)(2,1)S(1)} %broadcast_in_dim.24), channel_id=1, replica_groups=mesh['shard'=2,'ctx'=16,'tp'=4] {'tp'}, dimensions={0} | all-to-all | bytes 2097152 | tf_op jit(solution)/shard_map/all_to_all | solution.py:11
  249.3 5.4 %convolution_bitcast_fusion = f32[1152,1024]{0,1:T(8,128)} fusion(bf16[2,256,1152]{2,1,0:T(8,128)(2,1)} %get-tuple-element.24, bf16[2,256,1024]{2,1,0:T(8,128)(2,1)} %bitcast.162), kind=kOutput, calls=%fused_computation.1 | convolution fusion | flops 1207959552 | bytes 6946816 | tf_op jit(solution)/shard_map/jzo,jzh->oh/dot_general | solution.py:149
  254.9 1.6 fusion.31
  256.4 2.0 multiply_reduce_fusion.2
  263.0 2.6 convolution_bitcast_fusion.3
  265.7 3.8 fusion.2
  269.4 1.5 copy.112
  271.0 3.7 all-to-all-start.5
  274.7 2.5 fusion.13
  278.8 23.1 %all-to-all-done.5 = f32[4,2,256,256]{3,2,1,0:T(8,128)S(1)} async-done(((f32[4,2,256,256]{3,2,1,0:T(8,128)}), f32[4,2,256,256]{3,2,1,0:T(8,128)S(1)}, u32[]{:S(2)}, u32[]{:S(2)}) %all-to-all-start.5) | async-done | bytes 2097184 | tf_op jit(solution)/shard_map/all_to_all | solution.py:36
  301.8 4.5 all-to-all-start.10
  307.3 26.3 %all-to-all-done.10 = f32[4,2,256,256]{3,2,1,0:T(8,128)} async-done(((f32[4,2,256,256]{3,2,1,0:T(8,128)}), f32[4,2,256,256]{3,2,1,0:T(8,128)}, u32[]{:S(2)}, u32[]{:S(2)}) %all-to-all-start.10) | async-done | bytes 2097184 | tf_op jit(solution)/shard_map/all_to_all | solution.py:36
  333.6 1.8 reduce_sum.171
  336.3 3.2 all-to-all-start.11
  339.6 5.3 all-to-all-done.11
  345.6 5.4 all-to-all-start.12
  352.3 6.9 %all-to-all-done.12 = f32[32,1,1280]{2,1,0:T(1,128)S(1)} async-done(((f32[32,1,1280]{2,1,0:T(1,128)}), f32[32,1,1280]{2,1,0:T(1,128)S(1)}, u32[]{:S(2)}, u32[]{:S(2)}) %all-to-all-start.12) | async-done | bytes 163872 | tf_op jit(solution)/shard_map/all_to_all | solution.py:11
  360.5 1.7 fusion.43
  362.4 87.0 %reduce-scatter.11.cloned.1.call-done = f32[1152,32]{0,1:T(8,128)} async-done(((f32[1152,1024]{0,1:T(8,128)}), f32[1152,32]{0,1:T(8,128)}) %reduce-scatter.11.cloned.1.call-update) | async-done | bytes 147472 | tf_op jit(solution)/shard_map/reduce_scatter | solution.py:218
  449.4 84.4 %reduce-scatter.5.cloned.1.call-done = f32[32,3,256]{2,0,1:T(8,128)} async-done(((f32[1024,3,256]{2,0,1:T(8,128)}), f32[32,3,256]{2,0,1:T(8,128)}) %reduce-scatter.5.cloned.1.call-update) | async-done | bytes 98320 | tf_op jit(solution)/shard_map/reduce_scatter | solution.py:215
  (122 shorter events, 27.7 us)
Async XLA Ops:
  7.2 1.5 copy-start.2
  7.2 11.4 %copy-start.22 = (f32[256]{0:T(256)S(1)}, f32[256]{0:T(256)}, u32[]{:S(2)}) copy-start(f32[256]{0:T(256)} %param.16) | copy-start | bytes 3076
  7.2 36.2 %all-gather.5.cloned.1.call-start = ((), (), s32[]{:S(2)}) async-start(), calls=%async_computation.17 | async-start | bytes 2359296 | tf_op jit(solution)/shard_map/all_gather | solution.py:102
  7.9 121.6 %all-gather.11.cloned.1.call-start = ((), (), s32[]{:S(2)}) async-start(), calls=%async_computation.20 | async-start | bytes 3538944 | tf_op jit(solution)/shard_map/all_gather | solution.py:106
  18.7 5.3 copy-start.23
  19.8 17.4 %all-to-all-start.1 = ((bf16[4,2,256,256]{3,2,1,0:T(8,128)(2,1)}), bf16[4,2,256,256]{3,2,1,0:T(8,128)(2,1)S(1)}, u32[]{:S(2)}, u32[]{:S(2)}) async-start(bf16[4,2,256,256]{3,2,1,0:T(8,128)(2,1)} %broadcast_in_dim.19), calls=%async_computation.1 | async-start | bytes 2097152 | tf_op jit(solution)/shard_map/all_to_all | solution.py:11
  23.3 120.0 %all-gather.9.cloned.1.call-start = ((), (), s32[]{:S(2)}) async-start(), calls=%async_computation.19 | async-start | bytes 3538944 | tf_op jit(solution)/shard_map/all_gather | solution.py:105
  38.8 8.8 %copy-start.15 = (bf16[256,512]{1,0:T(8,128)(2,1)S(1)}, bf16[256,512]{1,0:T(8,128)(2,1)}, u32[]{:S(2)}) copy-start(bf16[256,512]{1,0:T(8,128)(2,1)} %param.12) | copy-start | bytes 786436
  45.8 13.4 %copy-start.3 = (f32[2,256,3,256]{3,1,2,0:T(8,128)}, f32[2,256,3,256]{3,1,2,0:T(8,128)S(1)}, u32[]{:S(2)}) copy-start(f32[2,256,3,256]{3,1,2,0:T(8,128)S(1)} %fusion.15) | copy-start | bytes 4718596
  45.9 12.3 %collective-permute-start = (bf16[2,2,256]{2,1,0:T(2,128)(2,1)S(1)}, bf16[2,2,256]{2,1,0:T(2,128)(2,1)S(1)}, u32[]{:S(2)}, u32[]{:S(2)}) collective-permute-start(bf16[2,2,256]{2,1,0:T(2,128)(2,1)S(1)} %slice.92), channel_id=1, source_target_pairs={{0,4},{4,8},{8,12},{12,16},{16,20},{20,24},{24,28},{28,32},{32,36}... | collective-permute-start | bytes 6152 | tf_op jit(solution)/shard_map/ppermute | solution.py:43
  58.1 1.5 copy-start.4
  59.2 2.0 copy-start.8
  61.2 32.0 %all-to-all-start.2 = ((f32[4,2,256,256]{3,2,1,0:T(8,128)}), f32[4,2,256,256]{3,2,1,0:T(8,128)}, u32[]{:S(2)}, u32[]{:S(2)}) async-start(f32[4,2,256,256]{3,2,1,0:T(8,128)} %bitcast.152), calls=%async_computation.2 | async-start | bytes 4194304 | tf_op jit(solution)/shard_map/all_to_all | solution.py:36
  65.6 101.4 %all-gather.7.cloned.1.call-start = ((), (), s32[]{:S(2)}) async-start(), calls=%async_computation.18 | async-start | bytes 3538944 | tf_op jit(solution)/shard_map/all_gather | solution.py:104
  66.2 36.7 %copy-start.5 = (bf16[2,256,256]{2,1,0:T(8,128)(2,1)S(1)}, bf16[2,256,256]{2,1,0:T(8,128)(2,1)}, u32[]{:S(2)}) copy-start(bf16[2,256,256]{2,1,0:T(8,128)(2,1)} %param.19) | copy-start | bytes 786436
  95.0 12.4 %copy-start.21 = (f32[256]{0:T(256)S(1)}, f32[256]{0:T(256)}, u32[]{:S(2)}) copy-start(f32[256]{0:T(256)} %param.17) | copy-start | bytes 3076
  103.9 18.0 %all-to-all-start.6 = ((bf16[4,2,256,256]{3,2,1,0:T(8,128)(2,1)}), bf16[4,2,256,256]{3,2,1,0:T(8,128)(2,1)S(1)}, u32[]{:S(2)}, u32[]{:S(2)}) async-start(bf16[4,2,256,256]{3,2,1,0:T(8,128)(2,1)} %broadcast_in_dim.22), calls=%async_computation.6 | async-start | bytes 2097152 | tf_op jit(solution)/shard_map/all_to_all | solution.py:11
  123.9 18.0 %all-to-all-start.4 = ((bf16[4,2,256,256]{3,2,1,0:T(8,128)(2,1)}), bf16[4,2,256,256]{3,2,1,0:T(8,128)(2,1)}, u32[]{:S(2)}, u32[]{:S(2)}) async-start(bf16[4,2,256,256]{3,2,1,0:T(8,128)(2,1)} %broadcast_in_dim.21), calls=%async_computation.4 | async-start | bytes 2097152 | tf_op jit(solution)/shard_map/all_to_all | solution.py:11
  128.2 232.4 %reduce-scatter.9.cloned.1.call-start = ((), (), s32[]{:S(2)}) async-start(), calls=%async_computation.23 | async-start | bytes 9732096 | tf_op jit(solution)/shard_map/reduce_scatter | solution.py:49
  173.5 1.6 copy-start.12
  173.5 1.6 copy-start.14
  185.6 176.7 %reduce-scatter.7.cloned.1.call-start = ((), (), s32[]{:S(2)}) async-start(), calls=%async_computation.22 | async-start | bytes 1081344 | tf_op jit(solution)/shard_map/reduce_scatter | solution.py:216
  185.7 3.7 copy-start.13
  185.7 3.7 copy-start.24
  221.7 9.9 %copy-start.6 = (bf16[2,256,256]{2,1,0:T(8,128)(2,1)S(1)}, bf16[2,256,256]{2,1,0:T(8,128)(2,1)}, u32[]{:S(2)}) copy-start(bf16[2,256,256]{2,1,0:T(8,128)(2,1)} %param.19) | copy-start | bytes 786436
  223.6 23.9 %copy-start = (f32[2,256,256]{2,1,0:T(8,128)}, f32[2,256,256]{2,1,0:T(8,128)S(1)}, u32[]{:S(2)}) copy-start(f32[2,256,256]{2,1,0:T(8,128)S(1)} %reduce_sum.168) | copy-start | bytes 1572868
  232.0 15.7 %copy-start.9 = (bf16[2,256,256]{2,1,0:T(8,128)(2,1)S(1)}, bf16[2,256,256]{2,1,0:T(8,128)(2,1)}, u32[]{:S(2)}) copy-start(bf16[2,256,256]{2,1,0:T(8,128)(2,1)} %copy-done.8) | copy-start | bytes 786436
  249.3 200.1 %reduce-scatter.11.cloned.1.call-start = ((), (), s32[]{:S(2)}) async-start(), calls=%async_computation.24 | async-start | bytes 4866048 | tf_op jit(solution)/shard_map/reduce_scatter | solution.py:218
  254.8 279.0 %reduce-scatter.5.cloned.1.call-start = ((), (), s32[]{:S(2)}) async-start(), calls=%async_computation.21 | async-start | bytes 3244032 | tf_op jit(solution)/shard_map/reduce_scatter | solution.py:215
  254.8 1.6 copy-start.10
  258.6 3.1 collective-permute-start.1
  260.5 2.6 copy-start.16
  263.0 2.6 copy-start.18
  263.0 2.6 copy-start.20
  271.0 3.8 copy-start.17
  271.0 3.8 copy-start.19
  271.0 30.9 %all-to-all-start.5 = ((f32[4,2,256,256]{3,2,1,0:T(8,128)}), f32[4,2,256,256]{3,2,1,0:T(8,128)S(1)}, u32[]{:S(2)}, u32[]{:S(2)}) async-start(f32[4,2,256,256]{3,2,1,0:T(8,128)} %bitcast.153), calls=%async_computation.5 | async-start | bytes 4194304 | tf_op jit(solution)/shard_map/all_to_all | solution.py:36
  301.8 31.7 %all-to-all-start.10 = ((f32[4,2,256,256]{3,2,1,0:T(8,128)}), f32[4,2,256,256]{3,2,1,0:T(8,128)}, u32[]{:S(2)}, u32[]{:S(2)}) async-start(f32[4,2,256,256]{3,2,1,0:T(8,128)} %bitcast.151), calls=%async_computation.10 | async-start | bytes 4194304 | tf_op jit(solution)/shard_map/all_to_all | solution.py:36
  307.3 43.8 %copy-start.1 = (f32[2,256,256]{2,1,0:T(8,128)S(1)}, f32[2,256,256]{2,1,0:T(8,128)}, u32[]{:S(2)}) copy-start(f32[2,256,256]{2,1,0:T(8,128)} %copy-done) | copy-start | bytes 1572868
  307.3 43.8 %copy-start.7 = (bf16[2,256,256]{2,1,0:T(8,128)(2,1)S(1)}, bf16[2,256,256]{2,1,0:T(8,128)(2,1)}, u32[]{:S(2)}) copy-start(bf16[2,256,256]{2,1,0:T(8,128)(2,1)} %param.19) | copy-start | bytes 786436
  307.3 43.8 %copy-start.11 = (f32[2,256,256]{2,1,0:T(8,128)S(1)}, f32[2,256,256]{2,1,0:T(8,128)}, u32[]{:S(2)}) copy-start(f32[2,256,256]{2,1,0:T(8,128)} %reduce_sum.167) | copy-start | bytes 1572868
  336.3 8.5 %all-to-all-start.11 = ((f32[4,2,256]{2,1,0:T(2,128)}), f32[4,2,256]{2,1,0:T(2,128)S(1)}, u32[]{:S(2)}, u32[]{:S(2)}) async-start(f32[4,2,256]{2,1,0:T(2,128)} %broadcast_in_dim.25), calls=%async_computation.11 | async-start | bytes 16384 | tf_op jit(solution)/shard_map/all_to_all | solution.py:11
  345.6 13.6 %all-to-all-start.12 = ((f32[32,1,1280]{2,1,0:T(1,128)}), f32[32,1,1280]{2,1,0:T(1,128)S(1)}, u32[]{:S(2)}, u32[]{:S(2)}) async-start(f32[32,1,1280]{2,1,0:T(1,128)} %broadcast_in_dim.26), calls=%async_computation.16 | async-start | bytes 327680 | tf_op jit(solution)/shard_map/all_to_all | solution.py:11
Sparse Core Ops, SparseCore 0:
  9.7 33.6 all-gather.4
  45.1 39.5 all-gather.10
  86.3 39.6 all-gather.8
  127.5 39.5 all-gather.6
  185.7 95.0 reduce-scatter.8
  285.1 77.1 reduce-scatter.6
  366.7 82.6 reduce-scatter.10
  454.0 79.7 reduce-scatter.4
where the time goes:
time: 542 us; the launch traced here: 541 us
  waiting for transfers between devices  322 us (59%)
  blocking collectives  81.6 us (15%)
  matrix products  47 us (9%)
  starting transfers between devices  36.1 us (7%)
  other arithmetic  21.4 us (4%)
  local copies, waits for them, and re-layouts  18 us (3%)
  between operations  14.7 us (3%)
    reduce_scatter x1, waiting for transfers between devices, on_device(): lax.psum_scatter(local_down_weight, ('shard', 'ctx'), scatter_dimension=1...  87 us
    reduce_scatter x1, waiting for transfers between devices, on_device(): lax.psum_scatter(local_input_weight, ('shard', 'ctx'), scatter_dimension=...  84.4 us
    all_to_all x3, waiting for transfers between devices, sent_and_summed(): lax.all_to_all(tiles, axis, split_axis=0, concat_axis=0, tiled=True)  76.3 us
    all_to_all x5, waiting for transfers between devices, from_everyone(): lax.all_to_all(jnp.broadcast_to(x[None], (count, *x.shape)), axis, 0, 0,...  46.3 us
    all_to_all x4, blocking collectives, from_everyone(): lax.all_to_all(jnp.broadcast_to(x[None], (count, *x.shape)), axis, 0, 0,...  40.6 us
    all_to_all x1, blocking collectives, sent_and_summed(): lax.all_to_all(tiles, axis, split_axis=0, concat_axis=0, tiled=True)  30.5 us
    all_to_all x5, starting transfers between devices, from_everyone(): lax.all_to_all(jnp.broadcast_to(x[None], (count, *x.shape)), axis, 0, 0,...  20 us
    all_gather x1, waiting for transfers between devices, on_device(): lax.all_gather(gate_proj, 'shard', axis=0, tiled=True)  19.1 us
  transfers between devices with their start and end apart: 18, of which 14 were waited for; matrix products, arithmetic and copies ran while one was open for 13% of the time, Pallas kernels for 0%

commit v1 on v0

v1 whole, which is shorter than its diff:
```python
import types

import jax
import jax.numpy as jnp
from jax import lax
from jax.experimental import pallas as pl
from jax.experimental.pallas import tpu as pltpu
from jax.sharding import PartitionSpec as P

EPS = 1e-05
MESH = pl.DeviceIdType.MESH
f32, bf16 = jnp.float32, jnp.bfloat16
WIDE, SEQ, TOK, CH, HID = 1024, 256, 512, 256, 1152
DOWN, GATE, UP, OUT, IN = range(5)
COLS = (HID, HID, HID, CH, 3 * CH)
RIGHT, LEFT, ACROSS, CORE, Z1, X1, Z3, X3, NEXT, PREV = range(10)
AHEAD, GATHER, SUM, TOTAL, GRAD, GAINS, EDGE, BACK, SMALL = range(9)
X, COT, Q, B = range(5, 9)
ORDERS = {
    DOWN: ((Z1, X1, Z3, X3), (Z3, X3, Z1, X1)),
    GATE: ((X1, Z1, X3, Z3), (X3, Z3, X1, Z1)),
    UP: ((Z1, X3, Z3, X1), (X1, Z3, X3, Z1)),
    OUT: ((Z3, X1, Z1, X3), (X3, Z1, X1, Z3)),
    IN: ((Z1, X1, Z3, X3), (X3, Z3, X1, Z1)),
}
OFFSETS = (0, 8, 12, 14)


def scratch():
    v = pltpu.VMEM
    shapes = dict(
        xg=v((TOK, WIDE), bf16),
        cg=v((TOK, WIDE), bf16),
        qg=v((TOK, WIDE), bf16),
        bg=v((TOK, WIDE), bf16),
        n1=v((TOK, WIDE), bf16),
        gains=v((8, WIDE), f32),
        r1=v((TOK, 1), f32),
        r2=v((TOK, 1), f32),
        col=v((2, TOK, 1), f32),
        wi=v((3, WIDE, CH), bf16),
        wo=v((CH, WIDE), bf16),
        wg=v((WIDE, HID), bf16),
        wu=v((WIDE, HID), bf16),
        wd=v((HID, WIDE), bf16),
        proj=v((3, TOK, CH), f32),
        mpad=v((2, SEQ + 8, CH), f32),
        hs=v((2, 16, CH), bf16),
        hr=v((2, 16, CH), bf16),
        conv=v((TOK, CH), f32),
        gated=v((TOK, CH), bf16),
        ys=v((4, 2, 3, SEQ, CH), bf16),
        yr=v((4, 2, 2, SEQ, CH), bf16),
        yo=v((4, 2, 2, SEQ // 2, CH), bf16),
        own=v((4, TOK, CH), f32),
        resid=v((TOK, CH), f32),
        tg=v((SEQ, HID), f32),
        tu=v((SEQ, HID), f32),
        td=v((SEQ, HID), f32),
        lanes=v((SEQ, 128), f32),
        hid=v((TOK, HID), bf16),
        eg=v((TOK, HID), bf16),
        eu=v((TOK, HID), bf16),
        dres=v((TOK, CH), f32),
        dpad=v((2, SEQ + 8, CH), f32),
        ds=v((2, 8, CH), f32),
        dr=v((2, 8, CH), f32),
        dproj=v((TOK, 3 * CH), bf16),
        rso=v((2, 2, 8, SEQ), f32),
        rsr=v((2, 2, 3, 8, SEQ), f32),
        sums=v((6, 8, CH), f32),
        sumr=v((5, 8, CH), f32),
        terms=[v((2, 2, 16, 16, n), bf16) for n in COLS],
        paired=[v((2, 16, 16, n), bf16) for n in COLS],
        came=[v((2, 15, 16, n), bf16) for n in COLS],
        ssem=pltpu.SemaphoreType.DMA((256,)),
        rsem=pltpu.SemaphoreType.DMA((256,)),
        lsem=pltpu.SemaphoreType.DMA((16,)),
    )
    return shapes


def nn(a, b):
    return jnp.dot(a, b, preferred_element_type=f32)


def nt(a, b):
    return lax.dot_general(a, b, (((1,), (1,)), ((), ())), preferred_element_type=f32)


def tn(a, b):
    return lax.dot_general(a, b, (((0,), (0,)), ((), ())), preferred_element_type=f32)


def row_of(lanes):
    ones = jnp.ones((8, lanes.shape[1]), f32)
    return lax.dot_general(
        ones, lanes, (((1,), (1,)), ((), ())), precision=lax.Precision.HIGHEST, preferred_element_type=f32
    )


def block_kernel(r, *refs):
    (x_hbm, cot_hbm, in_hbm, out_hbm, gate_hbm, up_hbm, down_hbm, mg, fg, taps) = refs[:10]
    (block_out, input_grad, g_in, g_out, g_gate, g_up, g_down, g_small) = refs[10:]
    grads = {DOWN: g_down, GATE: g_gate, UP: g_up, OUT: g_out, IN: g_in}
    ssem, rsem, lsem = r.ssem, r.rsem, r.lsem

    shard, ctx, t = lax.axis_index("shard"), lax.axis_index("ctx"), lax.axis_index("tp")
    core, z, x = ctx % 2, (ctx // 2) % 4, shard * 2 + ctx // 8

    def dev(xx, zz, cc, tt):
        return (xx // 2, (xx % 2) * 8 + zz * 2 + cc, tt)

    z1, z3, x1, x3 = z + 1 - 2 * (z % 2), 3 - z, x + 1 - 2 * (x % 2), 3 - x
    right, left, across = (t + 1) % 4, (t + 3) % 4, (t + 2) % 4
    to = {
        RIGHT: (shard, ctx, right),
        LEFT: (shard, ctx, left),
        ACROSS: (shard, ctx, across),
        CORE: dev(x, z, 1 - core, t),
        Z1: dev(x, z1, core, t),
        Z3: dev(x, z3, core, t),
        X1: dev(x1, z, core, t),
        X3: dev(x3, z, core, t),
        NEXT: (shard, (ctx + 1) % 16, t),
        PREV: (shard, (ctx + 15) % 16, t),
    }

    ids, sent, local = {}, [], {}
    gathered = {X: r.xg, COT: r.cg, Q: r.qg, B: r.bg}

    def number(key):
        return ids.setdefault(key, len(ids))

    def send(key, src, dst, where):
        n = number(key)
        copy = pltpu.make_async_remote_copy(
            src_ref=src,
            dst_ref=dst,
            send_sem=ssem.at[n],
            recv_sem=rsem.at[n],
            device_id=to[where],
            device_id_type=MESH,
        )
        copy.start()
        sent.append(copy)

    def arrived(key, dst):
        pltpu.make_async_copy(dst, dst, rsem.at[number(key)]).wait()

    def fetch(key, src, dst):
        copy = pltpu.make_async_copy(src, dst, lsem.at[len(local)])
        copy.start()
        local[key] = copy

    def part(n):
        return pl.ds(pl.multiple_of(n * CH, CH), CH)

    def rows_of(s):
        return pl.ds(s * SEQ, SEQ)

    weights = {
        IN: (in_hbm, r.wi, 512),
        OUT: (out_hbm, r.wo, 256),
        GATE: (gate_hbm, r.wg, 512),
        UP: (up_hbm, r.wu, 512),
        DOWN: (down_hbm, r.wd, HID),
    }

    def piece(w, half, first, count):
        whole = weights[w][1]
        if w == IN:
            return whole.at[:, pl.ds(pl.multiple_of(half * 512 + first, 32), count), :]
        if w in (GATE, UP):
            return whole.at[pl.ds(pl.multiple_of(half * 512 + first, 32), count), :]
        return whole.at[pl.ds(pl.multiple_of(first, 16), count), pl.ds(pl.multiple_of(half * 512, 512), 512)]

    def source(w, first, count):
        held = weights[w][0]
        at = pl.ds(pl.multiple_of(first, 16), count)
        return held.at[:, at, :] if w == IN else held.at[at, :]

    def quarter(w):
        return weights[w][2] // 4

    pair = z % 2

    def weight_own(w):
        fetch(w, weights[w][0], piece(w, shard, 0, weights[w][2]))

    def weight_cross(w):
        n = quarter(w)
        first = (pair * 2 + core) * n
        send((AHEAD, w, 0), source(w, first, n), piece(w, shard, first, n), X3)

    def weight_around(w):
        n = quarter(w)
        first = (pair * 2 + core) * n
        mine = piece(w, 1 - shard, first, n)
        arrived((AHEAD, w, 0), mine)
        a, b = piece(w, 1 - shard, first, n // 2), piece(w, 1 - shard, first + n // 2, n // 2)
        send((AHEAD, w, 1), a, a, Z1)
        send((AHEAD, w, 2), b, b, Z3)
        send((AHEAD, w, 3), mine, mine, CORE)

    def weight_share(w):
        n = quarter(w)
        first = ((1 - pair) * 2 + core) * n
        arrived((AHEAD, w, 1), piece(w, 1 - shard, first, n // 2))
        arrived((AHEAD, w, 2), piece(w, 1 - shard, first + n // 2, n // 2))
        other = piece(w, 1 - shard, first, n)
        send((AHEAD, w, 4), other, other, CORE)

    def weight_ready(w):
        n = quarter(w)
        arrived((AHEAD, w, 3), piece(w, 1 - shard, (pair * 2 + 1 - core) * n, n))
        arrived((AHEAD, w, 4), piece(w, 1 - shard, ((1 - pair) * 2 + 1 - core) * n, n))
        local[w].wait()

    def gather_start(name, src, s):
        whole = gathered[name]
        dst = whole.at[rows_of(s), part(t)]
        send((GATHER, name, s, 0), src, dst, RIGHT)
        send((GATHER, name, s, 1), src, dst, LEFT)

    def gather_relay(name, s):
        whole = gathered[name]
        arrived((GATHER, name, s, 0), whole.at[rows_of(s), part(left)])
        a = whole.at[pl.ds(s * SEQ, SEQ // 2), part(left)]
        send((GATHER, name, s, 2), a, a, RIGHT)
        arrived((GATHER, name, s, 1), whole.at[rows_of(s), part(right)])
        b = whole.at[pl.ds(s * SEQ + SEQ // 2, SEQ // 2), part(right)]
        send((GATHER, name, s, 3), b, b, LEFT)

    def gather_finish(name, s):
        whole = gathered[name]
        arrived((GATHER, name, s, 2), whole.at[pl.ds(s * SEQ, SEQ // 2), part(across)])
        arrived((GATHER, name, s, 3), whole.at[pl.ds(s * SEQ + SEQ // 2, SEQ // 2), part(across)])

    top, low = pl.ds(0, SEQ // 2), pl.ds(SEQ // 2, SEQ // 2)

    def sum_start(ph, s, block):
        ys, yr, yo = r.ys, r.yr, r.yo
        ys[ph, s, 2] = block(across).astype(bf16)
        send((SUM, ph, s, 0), ys.at[ph, s, 2, top], yo.at[ph, s, 0], RIGHT)
        send((SUM, ph, s, 1), ys.at[ph, s, 2, low], yo.at[ph, s, 1], LEFT)
        ys[ph, s, 0] = block(right).astype(bf16)
        send((SUM, ph, s, 2), ys.at[ph, s, 0, low], yr.at[ph, s, 0, low], RIGHT)
        ys[ph, s, 1] = block(left).astype(bf16)
        send((SUM, ph, s, 3), ys.at[ph, s, 1, top], yr.at[ph, s, 1, top], LEFT)
        r.own[ph, rows_of(s), :] = block(t)

    def sum_relay(ph, s):
        ys, yr, yo = r.ys, r.yr, r.yo
        arrived((SUM, ph, s, 0), yo.at[ph, s, 0])
        ys[ph, s, 0, top, :] = (ys[ph, s, 0, top, :].astype(f32) + yo[ph, s, 0].astype(f32)).astype(bf16)
        send((SUM, ph, s, 4), ys.at[ph, s, 0, top], yr.at[ph, s, 0, top], RIGHT)
        arrived((SUM, ph, s, 1), yo.at[ph, s, 1])
        ys[ph, s, 1, low, :] = (ys[ph, s, 1, low, :].astype(f32) + yo[ph, s, 1].astype(f32)).astype(bf16)
        send((SUM, ph, s, 5), ys.at[ph, s, 1, low], yr.at[ph, s, 1, low], LEFT)

    def sum_finish(ph, s):
        yr = r.yr
        arrived((SUM, ph, s, 2), yr.at[ph, s, 0, low])
        arrived((SUM, ph, s, 3), yr.at[ph, s, 1, top])
        arrived((SUM, ph, s, 4), yr.at[ph, s, 0, top])
        arrived((SUM, ph, s, 5), yr.at[ph, s, 1, low])

    def summed(ph, s, i, n):
        at = pl.ds(i, n)
        own = r.own[ph, pl.ds(s * SEQ + i, n), :]
        return own + r.yr[ph, s, 0, at, :].astype(f32) + r.yr[ph, s, 1, at, :].astype(f32)

    def totals_start(kind, s, lanes):
        r.rso[kind, s] = row_of(lanes)
        for slot, where in enumerate((RIGHT, LEFT, ACROSS)):
            send((TOTAL, kind, s, slot), r.rso.at[kind, s], r.rsr.at[kind, s, slot], where)

    def totals_finish(kind, s):
        total = r.rso[kind, s]
        for slot in range(3):
            arrived((TOTAL, kind, s, slot), r.rsr.at[kind, s, slot])
            total = total + r.rsr[kind, s, slot]
        r.col[kind, rows_of(s), :] = jnp.transpose(total)[:, 0:1]

    def grad_product(g, lhs, rhs):
        held, width = r.terms[g], COLS[g]

        @pl.loop(0, 4)
        def _(xp):
            a = lhs[:, part(xp)]
            hi, lo = (xp // 2 + x // 2) % 2, (xp + x) % 2
            bits = {X3: hi, X1: (lo + hi) % 2}
            for first in range(0, width, 256):
                n = min(256, width - first)
                value = tn(a, rhs[:, first : first + n]).astype(bf16)
                for zp in range(4):
                    zh, zl = (zp // 2 + z // 2) % 2, (zp + z) % 2
                    bits[Z3], bits[Z1] = zh, (zl + zh) % 2
                    for cp in range(2):
                        mine = (cp + core) % 2
                        for half in range(2):
                            pos = 0
                            for d in ORDERS[g][half]:
                                pos = 2 * pos + bits[d]
                            at = (zp * 2 + cp) * 32 + half * 16
                            held[mine, half, pos, :, first : first + n] = value[at : at + 16]

        send((GRAD, g), held.at[1], r.paired[g], CORE)

    def grad_send(g, stage):
        n = 8 >> stage
        for half in range(2):
            send(
                (GRAD, g, half, stage),
                r.terms[g].at[0, half, pl.ds(n, n)],
                r.came[g].at[half, pl.ds(OFFSETS[stage], n)],
                ORDERS[g][half][stage],
            )

    def grad_first(g):
        held, came = r.terms[g], r.paired[g]
        arrived((GRAD, g), came)

        @pl.loop(0, 16)
        def _(i):
            for half in range(2):
                held[0, half, i] = (held[0, half, i].astype(f32) + came[half, i].astype(f32)).astype(bf16)

        grad_send(g, 0)

    def grad_next(g, stage):
        held, came = r.terms[g], r.came[g]
        n = 16 >> stage
        first = OFFSETS[stage - 1]
        for half in range(2):
            arrived((GRAD, g, half, stage - 1), came.at[half, pl.ds(first, n)])

        @pl.loop(0, n)
        def _(i):
            for half in range(2):
                held[0, half, i] = (held[0, half, i].astype(f32) + came[half, first + i].astype(f32)).astype(bf16)

        grad_send(g, stage)

    def grad_last(g):
        held, came = r.terms[g], r.came[g]
        for half in range(2):
            arrived((GRAD, g, half, 3), came.at[half, pl.ds(14, 1)])
            total = held[0, half, 0].astype(f32) + came[half, 14].astype(f32)
            rows = pl.ds(half * 16, 16)
            if g == IN:
                for k in range(3):
                    g_in[k, rows, :] = total[:, k * CH : (k + 1) * CH]
            else:
                grads[g][rows, :] = total

    def in_rows(s, step, body):
        @pl.loop(0, SEQ // step)
        def _(n):
            i = pl.multiple_of(n * step, step)
            body(i, pl.ds(pl.multiple_of(s * SEQ + i, step), step))

    barrier = pltpu.get_barrier_semaphore()
    for where in to:
        pl.semaphore_signal(barrier, inc=1, device_id=to[where], device_id_type=MESH)
    fetch(X, x_hbm, r.xg.at[:, part(t)])
    fetch(COT, cot_hbm, r.cg.at[:, part(t)])
    for w in (IN, OUT, GATE, UP, DOWN):
        weight_own(w)
    own_gains = r.gains.at[:, part(t)]
    own_gains[...] = jnp.zeros((8, CH), f32)
    own_gains[0:1, :] = mg[...]
    own_gains[1:2, :] = fg[...]
    pl.semaphore_wait(barrier, len(to))

    for s in range(2):
        gather_start(X, x_hbm.at[rows_of(s)], s)
    for where in (RIGHT, LEFT, ACROSS):
        send((GAINS, where), own_gains, own_gains, where)
    for w in (IN, OUT, GATE, UP, DOWN):
        weight_cross(w)
    for s in range(2):
        gather_relay(X, s)
    for s in range(2):
        gather_start(COT, cot_hbm.at[rows_of(s)], s)
    weight_around(IN)
    local[X].wait()
    for where, block in ((RIGHT, left), (LEFT, right), (ACROSS, across)):
        arrived((GAINS, where), r.gains.at[:, part(block)])

    def normalise(s):
        def body(i, rows):
            v = r.xg[rows, :].astype(f32)
            scale = lax.rsqrt(jnp.sum(v * v, axis=1, keepdims=True) / WIDE + EPS)
            r.r1[rows, :] = scale
            r.n1[rows, :] = (v * scale * r.gains[0:1, :]).astype(bf16)

        in_rows(s, 32, body)

    def project(s):
        for k in range(3):
            r.proj[k, rows_of(s), :] = nn(r.n1[rows_of(s), :], r.wi[k])
        mixed = (r.proj[0, rows_of(s), :] * r.proj[2, rows_of(s), :]).astype(bf16)
        r.mpad[s, pl.ds(8, SEQ), :] = mixed.astype(f32)
        r.hs[s] = mixed[SEQ - 16 :]
        send((EDGE, s), r.hs.at[s], r.hr.at[s], NEXT)

    gather_finish(X, 0)
    normalise(0)
    gather_finish(X, 1)
    normalise(1)
    weight_share(IN)
    weight_around(OUT)
    weight_around(GATE)
    weight_ready(IN)
    project(0)
    project(1)
    weight_share(OUT)
    for s in range(2):
        gather_relay(COT, s)
    weight_around(UP)

    def branch(s):
        arrived((EDGE, s), r.hr.at[s])
        edge = r.hr[s].astype(f32)[8:16]
        r.mpad[s, 0:8, :] = jnp.where(ctx > 0, edge, 0.0)

        for i in range(0, SEQ, 64):
            rows = pl.ds(s * SEQ + i, 64)
            c = (
                taps[0:1, :] * r.mpad[s, i + 6 : i + 70, :]
                + taps[1:2, :] * r.mpad[s, i + 7 : i + 71, :]
                + taps[2:3, :] * r.mpad[s, i + 8 : i + 72, :]
            )
            r.conv[rows, :] = c
            r.gated[rows, :] = (r.proj[1, rows, :] * c).astype(bf16)

        sum_start(0, s, lambda n: nn(r.gated[rows_of(s), :], r.wo[:, part(n)]))

    weight_ready(OUT)
    branch(0)
    branch(1)
    sum_relay(0, 0)
    weight_share(GATE)
    sum_relay(0, 1)
    weight_around(DOWN)
    weight_share(UP)

    def second(s):
        sum_finish(0, s)

        def body(i, rows):
            value = r.xg[rows, part(t)].astype(f32) + summed(0, s, i, 32)
            r.resid[rows, :] = value
            r.qg[rows, part(t)] = (value * fg[...]).astype(bf16)

        in_rows(s, 32, body)
        gather_start(Q, r.qg.at[rows_of(s), part(t)], s)

    second(0)
    second(1)
    gather_relay(Q, 0)
    gather_relay(Q, 1)
    local[COT].wait()
    weight_share(DOWN)
    gather_finish(COT, 0)
    gather_finish(COT, 1)
    for w in (GATE, UP, DOWN):
        weight_ready(w)

    def feed(s):
        gather_finish(Q, s)

        def scales(i, rows):
            v = r.qg[rows, :].astype(f32) * (1.0 / r.gains[1:2, :])
            r.r2[rows, :] = lax.rsqrt(jnp.sum(v * v, axis=1, keepdims=True) / WIDE + EPS)

        in_rows(s, 32, scales)
        q, c = r.qg[rows_of(s), :], r.cg[rows_of(s), :]
        for first in range(0, HID, 256):
            cols = pl.ds(first, min(256, HID - first))
            r.tg[:, cols] = nn(q, r.wg[:, cols])
            r.tu[:, cols] = nn(q, r.wu[:, cols])
            r.td[:, cols] = nt(c, r.wd[cols, :])

        def body(i, rows):
            here = pl.ds(i, 16)
            scale = r.r2[rows, :]
            total = jnp.zeros((16, 128), f32)
            for first in range(0, HID, 384):
                cols = pl.ds(first, 384)
                gate, up, dh = r.tg[here, cols] * scale, r.tu[here, cols] * scale, r.td[here, cols]
                sg = jax.nn.sigmoid(gate)
                act = gate * sg
                r.hid[rows, cols] = (act * up).astype(bf16)
                d_gate = dh * up * sg * (1.0 + gate * (1.0 - sg))
                d_up = dh * act
                r.eg[rows, cols] = (d_gate * scale).astype(bf16)
                r.eu[rows, cols] = (d_up * scale).astype(bf16)
                both = d_gate * gate + d_up * up
                for j in range(0, 384, 128):
                    total = total + both[:, j : j + 128]
            r.lanes[here, :] = total

        in_rows(s, 16, body)
        sum_start(
            1,
            s,
            lambda n: nt(r.eg[rows_of(s), :], r.wg[part(n), :]) + nt(r.eu[rows_of(s), :], r.wu[part(n), :]),
        )
        totals_start(0, s, r.lanes[...])

    feed(0)
    feed(1)
    sum_relay(1, 0)
    grad_product(GATE, r.qg, r.eg)
    sum_relay(1, 1)

    small = r.sums.at[0]
    small[...] = jnp.zeros((8, CH), f32)

    def through_norm(s):
        sum_finish(1, s)
        totals_finish(0, s)

        def body(i, rows):
            g = summed(1, s, i, 32)
            value, scale = r.resid[rows, :], r.r2[rows, :]
            small[1:2, :] += jnp.sum(g * value, axis=0, keepdims=True)
            d = (
                r.cg[rows, part(t)].astype(f32)
                + fg[...] * g
                - value * (scale * scale * r.col[0, rows, :] * (1.0 / WIDE))
            )
            r.dres[rows, :] = d
            r.bg[rows, part(t)] = d.astype(bf16)

        in_rows(s, 32, body)
        gather_start(B, r.bg.at[rows_of(s), part(t)], s)

    through_norm(0)
    through_norm(1)
    grad_product(UP, r.qg, r.eu)
    gather_relay(B, 0)
    gather_relay(B, 1)
    grad_first(GATE)
    for s in range(2):
        sum_start(2, s, lambda n: nn(r.hid[rows_of(s), :], r.wd[:, part(n)]))

    def back(s):
        gather_finish(B, s)
        d = nt(r.bg[rows_of(s), :], r.wo[...])
        r.tg[:, 0:CH] = d
        for i in range(0, SEQ, 64):
            rows = pl.ds(s * SEQ + i, 64)
            d = r.tg[i : i + 64, 0:CH]
            d_conv = d * r.proj[1, rows, :]
            r.dpad[s, i : i + 64, :] = d_conv
            d_c = d * r.conv[rows, :]
            r.dproj[rows, CH : 2 * CH] = d_c.astype(bf16)
            for j in range(3):
                small[2 + j : 3 + j, :] += jnp.sum(
                    d_conv * r.mpad[s, i + 6 + j : i + 70 + j, :], axis=0, keepdims=True
                )
        r.ds[s] = r.dpad[s, 0:8, :]
        send((BACK, s), r.ds.at[s], r.dr.at[s], PREV)

    def mixer(s):
        arrived((BACK, s), r.dr.at[s])
        r.dpad[s, SEQ : SEQ + 8, :] = jnp.where(ctx < 15, r.dr[s], 0.0)
        for i in range(0, SEQ, 64):
            rows = pl.ds(s * SEQ + i, 64)
            d_mixed = (
                taps[2:3, :] * r.dpad[s, i : i + 64, :]
                + taps[1:2, :] * r.dpad[s, i + 1 : i + 65, :]
                + taps[0:1, :] * r.dpad[s, i + 2 : i + 66, :]
            )
            b, c, xi = r.proj[0, rows, :], r.proj[1, rows, :], r.proj[2, rows, :]
            d_b, d_x = (d_mixed * xi).astype(bf16), (d_mixed * b).astype(bf16)
            r.dproj[rows, 0:CH] = d_b
            r.dproj[rows, 2 * CH :] = d_x
            d_c = r.dproj[rows, CH : 2 * CH].astype(f32)
            both = d_b.astype(f32) * b + d_x.astype(f32) * xi + d_c * c
            r.lanes[i : i + 64, :] = both[:, 0:128] + both[:, 128:256]

        def term(n):
            total = nt(r.dproj[rows_of(s), 0:CH], r.wi[0, part(n), :])
            for k in (1, 2):
                total += nt(r.dproj[rows_of(s), k * CH : (k + 1) * CH], r.wi[k, part(n), :])
            return total

        sum_start(3, s, term)
        totals_start(1, s, r.lanes[...])

    grad_first(UP)
    back(0)
    back(1)
    grad_next(GATE, 1)
    mixer(0)
    mixer(1)
    grad_product(IN, r.n1, r.dproj)
    sum_relay(3, 0)
    sum_relay(3, 1)
    grad_next(UP, 1)
    grad_next(GATE, 2)
    grad_product(OUT, r.bg, r.gated)
    grad_product(DOWN, r.cg, r.hid)
    sum_relay(2, 0)
    sum_relay(2, 1)
    grad_first(IN)
    grad_first(OUT)
    grad_first(DOWN)
    grad_next(UP, 2)

    def finish(s):
        sum_finish(3, s)
        totals_finish(1, s)

        def body(i, rows):
            g = summed(3, s, i, 32)
            value, scale = r.xg[rows, part(t)].astype(f32), r.r1[rows, :]
            small[0:1, :] += jnp.sum(g * (value * scale), axis=0, keepdims=True)
            input_grad[rows, :] = (
                r.dres[rows, :]
                + scale * (mg[...] * g)
                - value * (scale * scale * r.col[1, rows, :] * (1.0 / WIDE))
            )

        in_rows(s, 32, body)

    finish(0)
    finish(1)
    hops = (CORE, Z1, Z3, X1, X3)

    def small_send(n):
        send((SMALL, n), r.sums.at[n], r.sumr.at[n], hops[n])

    def small_add(n):
        arrived((SMALL, n), r.sumr.at[n])
        r.sums[n + 1] = r.sums[n] + r.sumr[n]

    small_send(0)
    grad_next(IN, 1)
    grad_next(OUT, 1)
    grad_next(DOWN, 1)
    small_add(0)
    small_send(1)
    grad_next(GATE, 3)
    grad_next(UP, 3)
    small_add(1)
    small_send(2)
    grad_next(IN, 2)
    grad_next(OUT, 2)
    grad_next(DOWN, 2)
    for s in range(2):
        sum_finish(2, s)

        def body(i, rows):
            block_out[rows, :] = (r.resid[rows, :] + summed(2, s, i, 32)).astype(bf16)

        in_rows(s, 32, body)
    small_add(2)
    small_send(3)
    grad_last(GATE)
    grad_last(UP)
    grad_next(IN, 3)
    grad_next(OUT, 3)
    grad_next(DOWN, 3)
    small_add(3)
    small_send(4)
    grad_last(IN)
    grad_last(OUT)
    grad_last(DOWN)
    small_add(4)
    g_small[...] = r.sums[5]
    for copy in sent:
        copy.wait_send()


def on_device(block_input, in_proj, out_proj, gate_proj, up_proj, down_proj, mixer_gain, ffn_gain, conv_kernel, cotangent):
    shapes = scratch()

    def kernel(*refs):
        taken, held = refs[18:], {}
        count = 0
        for name, shape in shapes.items():
            if isinstance(shape, list):
                held[name] = taken[count : count + len(shape)]
                count += len(shape)
            else:
                held[name] = taken[count]
                count += 1
        block_kernel(types.SimpleNamespace(**held), *refs[:18])

    hbm, vmem = pl.BlockSpec(memory_space=pl.ANY), pl.BlockSpec(memory_space=pltpu.VMEM)
    out = jax.ShapeDtypeStruct
    (block_out, input_grad, g_in, g_out, g_gate, g_up, g_down, g_small) = pl.pallas_call(
        kernel,
        out_shape=(
            out((TOK, CH), bf16),
            out((TOK, CH), f32),
            out((3, 32, CH), f32),
            out((32, CH), f32),
            out((32, HID), f32),
            out((32, HID), f32),
            out((32, HID), f32),
            out((8, CH), f32),
        ),
        in_specs=[hbm] * 7 + [vmem] * 3,
        out_specs=[vmem] * 8,
        scratch_shapes=jax.tree.leaves(list(shapes.values())),
        compiler_params=pltpu.CompilerParams(
            collective_id=0, has_side_effects=True, vmem_limit_bytes=62 * 1024 * 1024
        ),
    )(
        block_input.reshape(TOK, CH),
        cotangent.reshape(TOK, CH),
        jnp.transpose(in_proj, (1, 0, 2)),
        out_proj,
        gate_proj,
        up_proj,
        down_proj,
        mixer_gain.reshape(1, CH),
        ffn_gain.reshape(1, CH),
        conv_kernel,
    )
    return (
        block_out.reshape(2, SEQ, CH),
        input_grad.reshape(2, SEQ, CH),
        jnp.transpose(g_in, (1, 0, 2)),
        g_out.T,
        g_gate,
        g_up,
        g_down.T,
        g_small[0],
        g_small[1],
        g_small[2:5],
    )


def solution(mesh):
    return jax.shard_map(
        on_device,
        mesh=mesh,
        in_specs=(
            P("shard", "ctx", "tp"),
            P("shard", None, "tp"),
            P("tp", "shard"),
            P("shard", "tp"),
            P("shard", "tp"),
            P("tp", "shard"),
            P("tp"),
            P("tp"),
            P(None, "tp"),
            P("shard", "ctx", "tp"),
        ),
        out_specs=(
            P("shard", "ctx", "tp"),
            P("shard", "ctx", "tp"),
            P(("shard", "ctx"), None, "tp"),
            P("tp", ("shard", "ctx")),
            P(("shard", "ctx"), "tp"),
            P(("shard", "ctx"), "tp"),
            P("tp", ("shard", "ctx")),
            P("tp"),
            P("tp"),
            P(None, "tp"),
        ),
        check_vma=False,
    )
```

time: 542 us -> 143 us (0.26)
  waiting for transfers between devices: 322 us -> 0 us
  Pallas kernels: 0 us -> 133 us
  blocking collectives: 81.6 us -> 0 us
  matrix products: 47 us -> 0 us
  starting transfers between devices: 36.1 us -> 0 us
  other arithmetic: 21.4 us -> 0 us
  between operations: 14.7 us -> 0.69 us
  local copies, waits for them, and re-layouts: 18 us -> 9.46 us
    reduce_scatter x4 -> x0, waiting for transfers between devices: 172 us -> none  [the longest x1 87 us: on_device(): lax.psum_scatter(local_down_weight, ('shard', 'ctx'), scatter_dimension=1...]
    pallas_call x0 -> x1, Pallas kernels: none -> 133 us  [on_device(): pl.pallas_call(kernel, out_shape=(out((TOK, CH), bf16), out((TOK, CH), f3...]
    all_to_all x8 -> x0, waiting for transfers between devices: 123 us -> none  [the longest x3 76.3 us: sent_and_summed(): lax.all_to_all(tiles, axis, split_axis=0, concat_axis=0, tiled=True)]
    all_to_all x5 -> x0, blocking collectives: 71.1 us -> none  [the longest x4 40.6 us: from_everyone(): lax.all_to_all(jnp.broadcast_to(x[None], (count, *x.shape)), axis, 0, 0,...]
    dot_general x15 -> x0, matrix products: 47 us -> none  [the longest x1 6.48 us: on_device(): jnp.einsum('zxw,wt->zxt', second_normalized, gate_weight, preferred_eleme...]
    all_to_all x8 -> x0, starting transfers between devices: 32.6 us -> none  [the longest x5 20 us: from_everyone(): lax.all_to_all(jnp.broadcast_to(x[None], (count, *x.shape)), axis, 0, 0,...]
    all_gather x4 -> x0, waiting for transfers between devices: 23.7 us -> none  [the longest x1 19.1 us: on_device(): lax.all_gather(gate_proj, 'shard', axis=0, tiled=True)]
    all_gather x1 -> x0, blocking collectives: 10.5 us -> none  [on_device(): lax.all_gather(out_proj, 'shard', axis=1, tiled=True)]
  transfers between devices with their start and end apart: 18 -> 0, of which waited for: 14 -> 0; matrix products, arithmetic and copies ran while one was open for 13% -> 0% of each run, Pallas kernels for 0% -> 0%
where the time goes in v1:
time: 143 us
  Pallas kernels  133 us (93%)
  local copies, waits for them, and re-layouts  9.46 us (7%)
    pallas_call x1, Pallas kernels, on_device(): pl.pallas_call(kernel, out_shape=(out((TOK, CH), bf16), out((TOK, CH), f3...  133 us
    unnamed x17, local copies, waits for them, and re-layouts  6.83 us

profile of v1, /device:TPU:0, one launch (start us, length us, event | category | flops | bytes accessed | tf_op | source)
XLA Modules:
  0.0 142.9 jit_solution(7658411254682858050)
XLA Ops:
  0.6 132.7 %shard_map.177 = (bf16[512,256]{1,0:T(8,128)(2,1)}, f32[512,256]{1,0:T(8,128)}, f32[3,32,256]{2,1,0:T(8,128)}, f32[32,256]{1,0:T(8,128)}, f32[32,1152]{1,0:T(8,1...) custom-call(bf16[512,256]{1,0:T(8,128)(2,1)} %bitcast.15, bf16[512,256]{1,0:T(8,128)(2,1)} %bitcast.16, ...), custom_call_target="tpu_custom_call" | custom-call | tf_op jit(solution)/shard_map/pallas_call | solution.py:698
  133.4 0.0 copy-start.3
  133.4 0.0 copy-start.4
  133.4 0.0 copy-start.2
  133.4 0.0 copy-start.1
  133.4 1.3 fusion
  134.8 1.3 slice.11
  136.1 0.0 copy-start
  136.1 1.7 %copy.27 = bf16[2,256,256]{2,1,0:T(8,128)(2,1)} copy(bf16[2,256,256]{2,1,0:T(8,128)(2,1)} %bitcast.14) | data formatting | bytes 524288
  137.8 1.9 %copy.28 = f32[2,256,256]{2,1,0:T(8,128)} copy(f32[2,256,256]{2,1,0:T(8,128)} %bitcast.13) | data formatting | bytes 1048576
  139.6 0.0 copy-done.3
  139.7 0.6 copy.29
  140.3 0.0 copy-done.4
  140.3 0.6 copy.30
  140.9 0.0 copy-done.2
  140.9 0.7 copy.31
  141.6 0.0 copy-done.1
  141.6 0.7 copy.32
  142.2 0.0 copy-done
  142.2 0.7 copy.33
Async XLA Ops:
  133.4 6.3 %copy-start.3 = (f32[3,32,256]{2,1,0:T(8,128)S(1)}, f32[3,32,256]{2,1,0:T(8,128)}, u32[]{:S(2)}) copy-start(f32[3,32,256]{2,1,0:T(8,128)} %get-tuple-element.20) | copy-start | bytes 294916
  133.4 6.9 %copy-start.4 = (f32[32,256]{1,0:T(8,128)S(1)}, f32[32,256]{1,0:T(8,128)}, u32[]{:S(2)}) copy-start(f32[32,256]{1,0:T(8,128)} %get-tuple-element.21) | copy-start | bytes 98308
  133.4 7.5 %copy-start.2 = (f32[32,1152]{1,0:T(8,128)S(1)}, f32[32,1152]{1,0:T(8,128)}, u32[]{:S(2)}) copy-start(f32[32,1152]{1,0:T(8,128)} %get-tuple-element.42) | copy-start | bytes 442372
  133.4 8.1 %copy-start.1 = (f32[32,1152]{1,0:T(8,128)S(1)}, f32[32,1152]{1,0:T(8,128)}, u32[]{:S(2)}) copy-start(f32[32,1152]{1,0:T(8,128)} %get-tuple-element.43) | copy-start | bytes 442372
  136.1 6.2 %copy-start = (f32[32,1152]{1,0:T(8,128)S(1)}, f32[32,1152]{1,0:T(8,128)}, u32[]{:S(2)}) copy-start(f32[32,1152]{1,0:T(8,128)} %get-tuple-element.24) | copy-start | bytes 442372

commit v2 on v1

--- a/solution.py
+++ b/solution.py
@@ -13,19 +13,9 @@
 WIDE, SEQ, TOK, CH, HID = 1024, 256, 512, 256, 1152
 DOWN, GATE, UP, OUT, IN = range(5)
 COLS = (HID, HID, HID, CH, 3 * CH)
-RIGHT, LEFT, ACROSS, CORE, Z1, X1, Z3, X3, NEXT, PREV = range(10)
+RIGHT, LEFT, ACROSS, CORE, Z1, X1, Z3, X3, NEXT, PREV, X2, Z2, Z1C, Z2C, Z3C = range(15)
 AHEAD, GATHER, SUM, TOTAL, GRAD, GAINS, EDGE, BACK, SMALL = range(9)
 X, COT, Q, B = range(5, 9)
-ORDERS = {
-    DOWN: ((Z1, X1, Z3, X3), (Z3, X3, Z1, X1)),
-    GATE: ((X1, Z1, X3, Z3), (X3, Z3, X1, Z1)),
-    UP: ((Z1, X3, Z3, X1), (X1, Z3, X3, Z1)),
-    OUT: ((Z3, X1, Z1, X3), (X3, Z1, X1, Z3)),
-    IN: ((Z1, X1, Z3, X3), (X3, Z3, X1, Z1)),
-}
-OFFSETS = (0, 8, 12, 14)
-
-
 def scratch():
     v = pltpu.VMEM
     shapes = dict(
@@ -50,8 +40,7 @@
         conv=v((TOK, CH), f32),
         gated=v((TOK, CH), bf16),
         ys=v((4, 2, 3, SEQ, CH), bf16),
-        yr=v((4, 2, 2, SEQ, CH), bf16),
-        yo=v((4, 2, 2, SEQ // 2, CH), bf16),
+        yr=v((4, 2, 3, SEQ, CH), bf16),
         own=v((4, TOK, CH), f32),
         resid=v((TOK, CH), f32),
         tg=v((SEQ, HID), f32),
@@ -68,14 +57,14 @@
         dproj=v((TOK, 3 * CH), bf16),
         rso=v((2, 2, 8, SEQ), f32),
         rsr=v((2, 2, 3, 8, SEQ), f32),
-        sums=v((6, 8, CH), f32),
-        sumr=v((5, 8, CH), f32),
+        sums=v((2, 8, CH), f32),
+        sumr=v((10, 8, CH), f32),
         terms=[v((2, 2, 16, 16, n), bf16) for n in COLS],
         paired=[v((2, 16, 16, n), bf16) for n in COLS],
         came=[v((2, 15, 16, n), bf16) for n in COLS],
-        ssem=pltpu.SemaphoreType.DMA((256,)),
-        rsem=pltpu.SemaphoreType.DMA((256,)),
-        lsem=pltpu.SemaphoreType.DMA((16,)),
+        ssem=pltpu.SemaphoreType.DMA((24,)),
+        rsem=pltpu.SemaphoreType.DMA((64,)),
+        lsem=pltpu.SemaphoreType.DMA((7,)),
     )
     return shapes
 
@@ -124,29 +113,32 @@
         X3: dev(x3, z, core, t),
         NEXT: (shard, (ctx + 1) % 16, t),
         PREV: (shard, (ctx + 15) % 16, t),
+        X2: dev((x + 2) % 4, z, core, t),
+        Z2: dev(x, (z + 2) % 4, core, t),
+        Z1C: dev(x, z1, 1 - core, t),
+        Z2C: dev(x, (z + 2) % 4, 1 - core, t),
+        Z3C: dev(x, z3, 1 - core, t),
     }
 
-    ids, sent, local = {}, [], {}
+    came_ids, sent_ids, local = {}, {}, {}
     gathered = {X: r.xg, COT: r.cg, Q: r.qg, B: r.bg}
 
-    def number(key):
-        return ids.setdefault(key, len(ids))
-
-    def send(key, src, dst, where):
-        n = number(key)
-        copy = pltpu.make_async_remote_copy(
+    def send(key, group, src, dst, where):
+        n, m = came_ids.setdefault(key, len(came_ids)), sent_ids.setdefault(group, len(sent_ids))
+        pltpu.make_async_remote_copy(
             src_ref=src,
             dst_ref=dst,
-            send_sem=ssem.at[n],
+            send_sem=ssem.at[m],
             recv_sem=rsem.at[n],
             device_id=to[where],
             device_id_type=MESH,
-        )
-        copy.start()
-        sent.append(copy)
-
-    def arrived(key, dst):
-        pltpu.make_async_copy(dst, dst, rsem.at[number(key)]).wait()
+        ).start()
+
+    def arrived(key, size):
+        pltpu.make_async_copy(size, size, rsem.at[came_ids[key]]).wait()
+
+    def left_all(group, size):
+        pltpu.make_async_copy(size, size, ssem.at[sent_ids[group]]).wait()
 
     def fetch(key, src, dst):
         copy = pltpu.make_async_copy(src, dst, lsem.at[len(local)])
@@ -191,7 +183,7 @@
     def weight_cross(w):
         n = quarter(w)
         first = (pair * 2 + core) * n
-        send((AHEAD, w, 0), source(w, first, n), piece(w, shard, first, n), X3)
+        send((AHEAD, w, 0), (AHEAD, w), source(w, first, n), piece(w, shard, first, n), X3)
 
     def weight_around(w):
         n = quarter(w)
@@ -199,87 +191,74 @@
         mine = piece(w, 1 - shard, first, n)
         arrived((AHEAD, w, 0), mine)
         a, b = piece(w, 1 - shard, first, n // 2), piece(w, 1 - shard, first + n // 2, n // 2)
-        send((AHEAD, w, 1), a, a, Z1)
-        send((AHEAD, w, 2), b, b, Z3)
-        send((AHEAD, w, 3), mine, mine, CORE)
+        send((AHEAD, w, 1), (AHEAD, w), a, a, Z1)
+        send((AHEAD, w, 1), (AHEAD, w), b, b, Z3)
+        send((AHEAD, w, 2), (AHEAD, w), mine, mine, CORE)
 
     def weight_share(w):
         n = quarter(w)
         first = ((1 - pair) * 2 + core) * n
-        arrived((AHEAD, w, 1), piece(w, 1 - shard, first, n // 2))
-        arrived((AHEAD, w, 2), piece(w, 1 - shard, first + n // 2, n // 2))
         other = piece(w, 1 - shard, first, n)
-        send((AHEAD, w, 4), other, other, CORE)
+        arrived((AHEAD, w, 1), other)
+        send((AHEAD, w, 2), (AHEAD, w), other, other, CORE)
 
     def weight_ready(w):
-        n = quarter(w)
-        arrived((AHEAD, w, 3), piece(w, 1 - shard, (pair * 2 + 1 - core) * n, n))
-        arrived((AHEAD, w, 4), piece(w, 1 - shard, ((1 - pair) * 2 + 1 - core) * n, n))
+        arrived((AHEAD, w, 2), piece(w, 1 - shard, 0, 2 * quarter(w)))
         local[w].wait()
 
+    others = ((ACROSS, across), (RIGHT, right), (LEFT, left))
+
     def gather_start(name, src, s):
+        dst = gathered[name].at[rows_of(s), part(t)]
+        for where, _ in others:
+            send((GATHER, name, s), GATHER, src, dst, where)
+
+    def gather_finish(name, s):
+        arrived((GATHER, name, s), r.ys.at[0, 0])
+
+    def ring_start(name, src, s):
+        dst = gathered[name].at[rows_of(s), part(t)]
+        send((GATHER, name, s, RIGHT), name, src, dst, RIGHT)
+        send((GATHER, name, s, LEFT), name, src, dst, LEFT)
+
+    def ring_relay(name, s):
         whole = gathered[name]
-        dst = whole.at[rows_of(s), part(t)]
-        send((GATHER, name, s, 0), src, dst, RIGHT)
-        send((GATHER, name, s, 1), src, dst, LEFT)
-
-    def gather_relay(name, s):
+        arrived((GATHER, name, s, RIGHT), whole.at[rows_of(s), part(left)])
+        a = whole.at[pl.ds(s * SEQ, SEQ // 2), part(left)]
+        send((GATHER, name, s, X1), name, a, a, RIGHT)
+        arrived((GATHER, name, s, LEFT), whole.at[rows_of(s), part(right)])
+        b = whole.at[pl.ds(s * SEQ + SEQ // 2, SEQ // 2), part(right)]
+        send((GATHER, name, s, X3), name, b, b, LEFT)
+
+    def ring_finish(name, s):
         whole = gathered[name]
-        arrived((GATHER, name, s, 0), whole.at[rows_of(s), part(left)])
-        a = whole.at[pl.ds(s * SEQ, SEQ // 2), part(left)]
-        send((GATHER, name, s, 2), a, a, RIGHT)
-        arrived((GATHER, name, s, 1), whole.at[rows_of(s), part(right)])
-        b = whole.at[pl.ds(s * SEQ + SEQ // 2, SEQ // 2), part(right)]
-        send((GATHER, name, s, 3), b, b, LEFT)
-
-    def gather_finish(name, s):
-        whole = gathered[name]
-        arrived((GATHER, name, s, 2), whole.at[pl.ds(s * SEQ, SEQ // 2), part(across)])
-        arrived((GATHER, name, s, 3), whole.at[pl.ds(s * SEQ + SEQ // 2, SEQ // 2), part(across)])
-
-    top, low = pl.ds(0, SEQ // 2), pl.ds(SEQ // 2, SEQ // 2)
+        arrived((GATHER, name, s, X1), whole.at[pl.ds(s * SEQ, SEQ // 2), part(across)])
+        arrived((GATHER, name, s, X3), whole.at[pl.ds(s * SEQ + SEQ // 2, SEQ // 2), part(across)])
 
     def sum_start(ph, s, block):
-        ys, yr, yo = r.ys, r.yr, r.yo
-        ys[ph, s, 2] = block(across).astype(bf16)
-        send((SUM, ph, s, 0), ys.at[ph, s, 2, top], yo.at[ph, s, 0], RIGHT)
-        send((SUM, ph, s, 1), ys.at[ph, s, 2, low], yo.at[ph, s, 1], LEFT)
-        ys[ph, s, 0] = block(right).astype(bf16)
-        send((SUM, ph, s, 2), ys.at[ph, s, 0, low], yr.at[ph, s, 0, low], RIGHT)
-        ys[ph, s, 1] = block(left).astype(bf16)
-        send((SUM, ph, s, 3), ys.at[ph, s, 1, top], yr.at[ph, s, 1, top], LEFT)
+        for slot, (where, n) in enumerate(others):
+            r.ys[ph, s, slot] = block(n).astype(bf16)
+            send((SUM, ph, s), SUM, r.ys.at[ph, s, slot], r.yr.at[ph, s, slot], where)
         r.own[ph, rows_of(s), :] = block(t)
 
-    def sum_relay(ph, s):
-        ys, yr, yo = r.ys, r.yr, r.yo
-        arrived((SUM, ph, s, 0), yo.at[ph, s, 0])
-        ys[ph, s, 0, top, :] = (ys[ph, s, 0, top, :].astype(f32) + yo[ph, s, 0].astype(f32)).astype(bf16)
-        send((SUM, ph, s, 4), ys.at[ph, s, 0, top], yr.at[ph, s, 0, top], RIGHT)
-        arrived((SUM, ph, s, 1), yo.at[ph, s, 1])
-        ys[ph, s, 1, low, :] = (ys[ph, s, 1, low, :].astype(f32) + yo[ph, s, 1].astype(f32)).astype(bf16)
-        send((SUM, ph, s, 5), ys.at[ph, s, 1, low], yr.at[ph, s, 1, low], LEFT)
-
     def sum_finish(ph, s):
-        yr = r.yr
-        arrived((SUM, ph, s, 2), yr.at[ph, s, 0, low])
-        arrived((SUM, ph, s, 3), yr.at[ph, s, 1, top])
-        arrived((SUM, ph, s, 4), yr.at[ph, s, 0, top])
-        arrived((SUM, ph, s, 5), yr.at[ph, s, 1, low])
+        arrived((SUM, ph, s), r.yr.at[ph, s])
 
     def summed(ph, s, i, n):
-        at = pl.ds(i, n)
-        own = r.own[ph, pl.ds(s * SEQ + i, n), :]
-        return own + r.yr[ph, s, 0, at, :].astype(f32) + r.yr[ph, s, 1, at, :].astype(f32)
+        total = r.own[ph, pl.ds(s * SEQ + i, n), :]
+        for slot in range(3):
+            total = total + r.yr[ph, s, slot, pl.ds(i, n), :].astype(f32)
+        return total
 
     def totals_start(kind, s, lanes):
         r.rso[kind, s] = row_of(lanes)
         for slot, where in enumerate((RIGHT, LEFT, ACROSS)):
-            send((TOTAL, kind, s, slot), r.rso.at[kind, s], r.rsr.at[kind, s, slot], where)
+            send((TOTAL, kind, s), TOTAL, r.rso.at[kind, s], r.rsr.at[kind, s, slot], where)
 
     def totals_finish(kind, s):
         total = r.rso[kind, s]
+        arrived((TOTAL, kind, s), r.rsr.at[kind, s])
         for slot in range(3):
-            arrived((TOTAL, kind, s, slot), r.rsr.at[kind, s, slot])
             total = total + r.rsr[kind, s, slot]
         r.col[kind, rows_of(s), :] = jnp.transpose(total)[:, 0:1]
 
@@ -289,65 +268,70 @@
         @pl.loop(0, 4)
         def _(xp):
             a = lhs[:, part(xp)]
-            hi, lo = (xp // 2 + x // 2) % 2, (xp + x) % 2
-            bits = {X3: hi, X1: (lo + hi) % 2}
+            xr = 2 * ((xp // 2 + x // 2) % 2) + (xp + x) % 2
             for first in range(0, width, 256):
                 n = min(256, width - first)
                 value = tn(a, rhs[:, first : first + n]).astype(bf16)
                 for zp in range(4):
-                    zh, zl = (zp // 2 + z // 2) % 2, (zp + z) % 2
-                    bits[Z3], bits[Z1] = zh, (zl + zh) % 2
+                    zr = 2 * ((zp // 2 + z // 2) % 2) + (zp + z) % 2
                     for cp in range(2):
                         mine = (cp + core) % 2
-                        for half in range(2):
-                            pos = 0
-                            for d in ORDERS[g][half]:
-                                pos = 2 * pos + bits[d]
-                            at = (zp * 2 + cp) * 32 + half * 16
-                            held[mine, half, pos, :, first : first + n] = value[at : at + 16]
-
-        send((GRAD, g), held.at[1], r.paired[g], CORE)
-
-    def grad_send(g, stage):
-        n = 8 >> stage
-        for half in range(2):
-            send(
-                (GRAD, g, half, stage),
-                r.terms[g].at[0, half, pl.ds(n, n)],
-                r.came[g].at[half, pl.ds(OFFSETS[stage], n)],
-                ORDERS[g][half][stage],
-            )
+                        at = (zp * 2 + cp) * 32
+                        held[mine, 0, 4 * zr + xr, :, first : first + n] = value[at : at + 16]
+                        held[mine, 1, 4 * xr + zr, :, first : first + n] = value[at + 16 : at + 32]
+
+        send((GRAD, g, 0), (GRAD, g, 0), held.at[1], r.paired[g], CORE)
+
+    routes = (((Z1, Z2, Z3), (X1, X2, X3)), ((X1, X2, X3), (Z1, Z2, Z3)))
 
     def grad_first(g):
         held, came = r.terms[g], r.paired[g]
-        arrived((GRAD, g), came)
+        arrived((GRAD, g, 0), came)
 
         @pl.loop(0, 16)
         def _(i):
             for half in range(2):
                 held[0, half, i] = (held[0, half, i].astype(f32) + came[half, i].astype(f32)).astype(bf16)
 
-        grad_send(g, 0)
-
-    def grad_next(g, stage):
+        for n in (2, 1, 3):
+            for half in range(2):
+                send(
+                    (GRAD, g, 1),
+                    (GRAD, g, 1),
+                    held.at[0, half, pl.ds(4 * n, 4)],
+                    r.came[g].at[half, pl.ds(4 * n - 4, 4)],
+                    routes[half][0][n - 1],
+                )
+
+    def grad_second(g):
         held, came = r.terms[g], r.came[g]
-        n = 16 >> stage
-        first = OFFSETS[stage - 1]
-        for half in range(2):
-            arrived((GRAD, g, half, stage - 1), came.at[half, pl.ds(first, n)])
-
-        @pl.loop(0, n)
+        arrived((GRAD, g, 1), came.at[:, pl.ds(0, 12)])
+
+        @pl.loop(0, 4)
         def _(i):
             for half in range(2):
-                held[0, half, i] = (held[0, half, i].astype(f32) + came[half, first + i].astype(f32)).astype(bf16)
-
-        grad_send(g, stage)
+                total = held[0, half, i].astype(f32)
+                for n in range(3):
+                    total = total + came[half, 4 * n + i].astype(f32)
+                held[0, half, i] = total.astype(bf16)
+
+        for n in (2, 1, 3):
+            for half in range(2):
+                send(
+                    (GRAD, g, 2),
+                    (GRAD, g, 1),
+                    held.at[0, half, pl.ds(n, 1)],
+                    came.at[half, pl.ds(11 + n, 1)],
+                    routes[half][1][n - 1],
+                )
 
     def grad_last(g):
         held, came = r.terms[g], r.came[g]
+        arrived((GRAD, g, 2), came.at[:, pl.ds(12, 3)])
         for half in range(2):
-            arrived((GRAD, g, half, 3), came.at[half, pl.ds(14, 1)])
-            total = held[0, half, 0].astype(f32) + came[half, 14].astype(f32)
+            total = held[0, half, 0].astype(f32)
+            for n in range(12, 15):
+                total = total + came[half, n].astype(f32)
             rows = pl.ds(half * 16, 16)
             if g == IN:
                 for k in range(3):
@@ -374,20 +358,16 @@
     own_gains[1:2, :] = fg[...]
     pl.semaphore_wait(barrier, len(to))
 
-    for s in range(2):
-        gather_start(X, x_hbm.at[rows_of(s)], s)
+    weight_cross(IN)
+    gather_start(X, x_hbm.at[rows_of(0)], 0)
     for where in (RIGHT, LEFT, ACROSS):
-        send((GAINS, where), own_gains, own_gains, where)
-    for w in (IN, OUT, GATE, UP, DOWN):
+        send(GAINS, GAINS, own_gains, own_gains, where)
+    gather_start(X, x_hbm.at[rows_of(1)], 1)
+    for w in (OUT, GATE, UP, DOWN):
         weight_cross(w)
     for s in range(2):
-        gather_relay(X, s)
-    for s in range(2):
-        gather_start(COT, cot_hbm.at[rows_of(s)], s)
+        ring_start(COT, cot_hbm.at[rows_of(s)], s)
     weight_around(IN)
-    local[X].wait()
-    for where, block in ((RIGHT, left), (LEFT, right), (ACROSS, across)):
-        arrived((GAINS, where), r.gains.at[:, part(block)])
 
     def normalise(s):
         def body(i, rows):
@@ -404,22 +384,21 @@
         mixed = (r.proj[0, rows_of(s), :] * r.proj[2, rows_of(s), :]).astype(bf16)
         r.mpad[s, pl.ds(8, SEQ), :] = mixed.astype(f32)
         r.hs[s] = mixed[SEQ - 16 :]
-        send((EDGE, s), r.hs.at[s], r.hr.at[s], NEXT)
-
+        send((EDGE, s), EDGE, r.hs.at[s], r.hr.at[s], NEXT)
+
+    local[X].wait()
+    arrived(GAINS, r.rsr.at[0, 0])
     gather_finish(X, 0)
     normalise(0)
+    weight_share(IN)
+    weight_around(OUT)
+    weight_ready(IN)
+    project(0)
     gather_finish(X, 1)
     normalise(1)
-    weight_share(IN)
-    weight_around(OUT)
-    weight_around(GATE)
-    weight_ready(IN)
-    project(0)
     project(1)
     weight_share(OUT)
-    for s in range(2):
-        gather_relay(COT, s)
-    weight_around(UP)
+    weight_around(GATE)
 
     def branch(s):
         arrived((EDGE, s), r.hr.at[s])
@@ -441,11 +420,10 @@
     weight_ready(OUT)
     branch(0)
     branch(1)
-    sum_relay(0, 0)
+    ring_relay(COT, 0)
+    ring_relay(COT, 1)
+    weight_around(UP)
     weight_share(GATE)
-    sum_relay(0, 1)
-    weight_around(DOWN)
-    weight_share(UP)
 
     def second(s):
         sum_finish(0, s)
@@ -460,14 +438,9 @@
 
     second(0)
     second(1)
-    gather_relay(Q, 0)
-    gather_relay(Q, 1)
+    weight_around(DOWN)
+    weight_share(UP)
     local[COT].wait()
-    weight_share(DOWN)
-    gather_finish(COT, 0)
-    gather_finish(COT, 1)
-    for w in (GATE, UP, DOWN):
-        weight_ready(w)
 
     def feed(s):
         gather_finish(Q, s)
@@ -477,11 +450,22 @@
             r.r2[rows, :] = lax.rsqrt(jnp.sum(v * v, axis=1, keepdims=True) / WIDE + EPS)
 
         in_rows(s, 32, scales)
-        q, c = r.qg[rows_of(s), :], r.cg[rows_of(s), :]
-        for first in range(0, HID, 256):
-            cols = pl.ds(first, min(256, HID - first))
+        if s == 0:
+            weight_ready(GATE)
+        q = r.qg[rows_of(s), :]
+        slices = [pl.ds(first, min(256, HID - first)) for first in range(0, HID, 256)]
+        for cols in slices:
             r.tg[:, cols] = nn(q, r.wg[:, cols])
+        if s == 0:
+            weight_share(DOWN)
+            weight_ready(UP)
+        for cols in slices:
             r.tu[:, cols] = nn(q, r.wu[:, cols])
+        ring_finish(COT, s)
+        if s == 0:
+            weight_ready(DOWN)
+        c = r.cg[rows_of(s), :]
+        for cols in slices:
             r.td[:, cols] = nt(c, r.wd[cols, :])
 
         def body(i, rows):
@@ -513,9 +497,6 @@
 
     feed(0)
     feed(1)
-    sum_relay(1, 0)
-    grad_product(GATE, r.qg, r.eg)
-    sum_relay(1, 1)
 
     small = r.sums.at[0]
     small[...] = jnp.zeros((8, CH), f32)
@@ -540,13 +521,15 @@
         gather_start(B, r.bg.at[rows_of(s), part(t)], s)
 
     through_norm(0)
+    grad_product(GATE, r.qg, r.eg)
+    grad_product(UP, r.qg, r.eu)
     through_norm(1)
-    grad_product(UP, r.qg, r.eu)
-    gather_relay(B, 0)
-    gather_relay(B, 1)
+
+    def deliver(s):
+        sum_start(2, s, lambda n: nn(r.hid[rows_of(s), :], r.wd[:, part(n)]))
+
+    deliver(0)
     grad_first(GATE)
-    for s in range(2):
-        sum_start(2, s, lambda n: nn(r.hid[rows_of(s), :], r.wd[:, part(n)]))
 
     def back(s):
         gather_finish(B, s)
@@ -564,7 +547,7 @@
                     d_conv * r.mpad[s, i + 6 + j : i + 70 + j, :], axis=0, keepdims=True
                 )
         r.ds[s] = r.dpad[s, 0:8, :]
-        send((BACK, s), r.ds.at[s], r.dr.at[s], PREV)
+        send((BACK, s), BACK, r.ds.at[s], r.dr.at[s], PREV)
 
     def mixer(s):
         arrived((BACK, s), r.dr.at[s])
@@ -593,25 +576,19 @@
         sum_start(3, s, term)
         totals_start(1, s, r.lanes[...])
 
+    back(0)
+    grad_product(DOWN, r.cg, r.hid)
     grad_first(UP)
-    back(0)
+    mixer(0)
     back(1)
-    grad_next(GATE, 1)
-    mixer(0)
+    grad_product(OUT, r.bg, r.gated)
+    grad_second(GATE)
+    grad_first(DOWN)
     mixer(1)
     grad_product(IN, r.n1, r.dproj)
-    sum_relay(3, 0)
-    sum_relay(3, 1)
-    grad_next(UP, 1)
-    grad_next(GATE, 2)
-    grad_product(OUT, r.bg, r.gated)
-    grad_product(DOWN, r.cg, r.hid)
-    sum_relay(2, 0)
-    sum_relay(2, 1)
-    grad_first(IN)
+    deliver(1)
+    grad_second(UP)
     grad_first(OUT)
-    grad_first(DOWN)
-    grad_next(UP, 2)
 
     def finish(s):
         sum_finish(3, s)
@@ -630,29 +607,14 @@
         in_rows(s, 32, body)
 
     finish(0)
+    grad_first(IN)
+    grad_second(DOWN)
+    grad_last(GATE)
     finish(1)
-    hops = (CORE, Z1, Z3, X1, X3)
-
-    def small_send(n):
-        send((SMALL, n), r.sums.at[n], r.sumr.at[n], hops[n])
-
-    def small_add(n):
-        arrived((SMALL, n), r.sumr.at[n])
-        r.sums[n + 1] = r.sums[n] + r.sumr[n]
-
-    small_send(0)
-    grad_next(IN, 1)
-    grad_next(OUT, 1)
-    grad_next(DOWN, 1)
-    small_add(0)
-    small_send(1)
-    grad_next(GATE, 3)
-    grad_next(UP, 3)
-    small_add(1)
-    small_send(2)
-    grad_next(IN, 2)
-    grad_next(OUT, 2)
-    grad_next(DOWN, 2)
+    for n, where in enumerate((CORE, Z1, Z2, Z3, Z1C, Z2C, Z3C)):
+        send((SMALL, 0), SMALL, r.sums.at[0], r.sumr.at[n], where)
+    grad_second(OUT)
+    grad_last(UP)
     for s in range(2):
         sum_finish(2, s)
 
@@ -660,22 +622,52 @@
             block_out[rows, :] = (r.resid[rows, :] + summed(2, s, i, 32)).astype(bf16)
 
         in_rows(s, 32, body)
-    small_add(2)
-    small_send(3)
-    grad_last(GATE)
-    grad_last(UP)
-    grad_next(IN, 3)
-    grad_next(OUT, 3)
-    grad_next(DOWN, 3)
-    small_add(3)
-    small_send(4)
+    total = r.sums[0]
+    arrived((SMALL, 0), r.sumr.at[pl.ds(0, 7)])
+    for n in range(7):
+        total = total + r.sumr[n]
+    r.sums[1] = total
+    for n, where in enumerate((X1, X2, X3)):
+        send((SMALL, 1), SMALL, r.sums.at[1], r.sumr.at[7 + n], where)
+    grad_second(IN)
+    grad_last(DOWN)
+    grad_last(OUT)
+    arrived((SMALL, 1), r.sumr.at[pl.ds(7, 3)])
+    for n in range(7, 10):
+        total = total + r.sumr[n]
+    g_small[...] = total
     grad_last(IN)
-    grad_last(OUT)
-    grad_last(DOWN)
-    small_add(4)
-    g_small[...] = r.sums[5]
-    for copy in sent:
-        copy.wait_send()
+
+    left_all(SUM, r.ys)
+    left_all(GATHER, r.ys.at[pl.ds(0, 3)])
+    left_all(COT, r.ys.at[0])
+    left_all(TOTAL, r.rsr)
+    left_all(GAINS, r.rsr.at[0, 0])
+    left_all(SMALL, r.sumr)
+    left_all(EDGE, r.hr)
+    left_all(BACK, r.dr)
+    for w in (IN, OUT, GATE, UP, DOWN):
+        left_all((AHEAD, w), piece(w, 0, 0, weights[w][2]))
+        left_all((GRAD, w, 0), r.paired[w])
+        left_all((GRAD, w, 1), r.came[w])
+
+
+def deliver_kernel(*refs):
+    small, whole = refs[0], refs[1:8]
+    ends, sums = refs[8:15], refs[15:18]
+    held, sem = refs[18:25], refs[25]
+    taken = [pltpu.make_async_copy(a, b, sem.at[0, n]) for n, (a, b) in enumerate(zip(whole, held))]
+    copies = [pltpu.make_async_copy(a, b, sem.at[1, n]) for n, (a, b) in enumerate(zip(held, ends))]
+    for copy in taken:
+        copy.start()
+    for first, then in zip(taken, copies):
+        first.wait()
+        then.start()
+    sums[0][...] = small[0]
+    sums[1][...] = small[1]
+    sums[2][...] = small[2:5]
+    for copy in copies:
+        copy.wait()
 
 
 def on_device(block_input, in_proj, out_proj, gate_proj, up_proj, down_proj, mixer_gain, ffn_gain, conv_kernel, cotangent):
@@ -695,7 +687,7 @@
 
     hbm, vmem = pl.BlockSpec(memory_space=pl.ANY), pl.BlockSpec(memory_space=pltpu.VMEM)
     out = jax.ShapeDtypeStruct
-    (block_out, input_grad, g_in, g_out, g_gate, g_up, g_down, g_small) = pl.pallas_call(
+    *whole, small = pl.pallas_call(
         kernel,
         out_shape=(
             out((TOK, CH), bf16),
@@ -725,6 +717,18 @@
         ffn_gain.reshape(1, CH),
         conv_kernel,
     )
+    block_out, input_grad, g_in, g_out, g_gate, g_up, g_down, mixer_sum, ffn_sum, taps_sum = pl.pallas_call(
+        deliver_kernel,
+        out_shape=(
+            *(out(a.shape, a.dtype) for a in whole),
+            out((CH,), f32),
+            out((CH,), f32),
+            out((3, CH), f32),
+        ),
+        in_specs=[vmem] + [hbm] * 7,
+        out_specs=[hbm] * 7 + [vmem] * 3,
+        scratch_shapes=[pltpu.VMEM(a.shape, a.dtype) for a in whole] + [pltpu.SemaphoreType.DMA((2, 7))],
+    )(small, *whole)
     return (
         block_out.reshape(2, SEQ, CH),
         input_grad.reshape(2, SEQ, CH),
@@ -733,9 +737,9 @@
         g_gate,
         g_up,
         g_down.T,
-        g_small[0],
-        g_small[1],
-        g_small[2:5],
+        mixer_sum,
+        ffn_sum,
+        taps_sum,
     )
 
 

time: 143 us -> 119 us (0.83)
  Pallas kernels: 133 us -> 117 us
  local copies, waits for them, and re-layouts: 9.46 us -> 0 us
    pallas_call x1, Pallas kernels: 133 us -> 114 us  [on_device(): pl.pallas_call(kernel, out_shape=(out((TOK, CH), bf16), out((TOK, CH), f3...]
    unnamed x17 -> x0, local copies, waits for them, and re-layouts: 6.83 us -> none
    pallas_call x0 -> x1, Pallas kernels: none -> 3.52 us  [on_device(): pl.pallas_call(deliver_kernel, out_shape=(*(out(a.shape, a.dtype) for a i...]
    slice x2 -> x0, local copies, waits for them, and re-layouts: 2.63 us -> none  [the longest x1 1.34 us: on_device(): g_small[1]]
where the time goes in v2:
time: 119 us; the launch traced here: 118 us
  Pallas kernels  117 us (98%)
    pallas_call x1, Pallas kernels, on_device(): pl.pallas_call(kernel, out_shape=(out((TOK, CH), bf16), out((TOK, CH), f3...  114 us
    pallas_call x1, Pallas kernels, on_device(): pl.pallas_call(deliver_kernel, out_shape=(*(out(a.shape, a.dtype) for a i...  3.52 us

profile of v2, /device:TPU:0, one launch (start us, length us, event | category | flops | bytes accessed | tf_op | source)
XLA Modules:
  0.0 118.1 jit_solution(12717741843007640232)
XLA Ops:
  0.6 113.8 %shard_map.177 = (bf16[512,256]{1,0:T(8,128)(2,1)}, f32[512,256]{1,0:T(8,128)}, f32[3,32,256]{2,1,0:T(8,128)}, f32[32,256]{1,0:T(8,128)}, f32[32,1152]{1,0:T(8,1...) custom-call(bf16[512,256]{1,0:T(8,128)(2,1)} %bitcast.11, bf16[512,256]{1,0:T(8,128)(2,1)} %bitcast.12, ...), custom_call_target="tpu_custom_call" | custom-call | tf_op jit(solution)/shard_map/pallas_call | solution.py:690
  114.4 3.5 %shard_map.178 = (bf16[512,256]{1,0:T(8,128)(2,1)}, f32[512,256]{1,0:T(8,128)}, f32[3,32,256]{2,1,0:T(8,128)}, f32[32,256]{1,0:T(8,128)}, f32[32,1152]{1,0:T(8,1...) custom-call(f32[8,256]{1,0:T(8,128)} %get-tuple-element.28.refs_0_, ...), custom_call_target="tpu_custom_call" | custom-call | tf_op jit(solution)/shard_map/pallas_call | solution.py:720

commit v3 on v2

--- a/solution.py
+++ b/solution.py
@@ -15,7 +15,7 @@
 COLS = (HID, HID, HID, CH, 3 * CH)
 RIGHT, LEFT, ACROSS, CORE, Z1, X1, Z3, X3, NEXT, PREV, X2, Z2, Z1C, Z2C, Z3C = range(15)
 AHEAD, GATHER, SUM, TOTAL, GRAD, GAINS, EDGE, BACK, SMALL = range(9)
-X, COT, Q, B = range(5, 9)
+X, COT, Q, B = range(20, 24)
 def scratch():
     v = pltpu.VMEM
     shapes = dict(
@@ -206,7 +206,7 @@
         arrived((AHEAD, w, 2), piece(w, 1 - shard, 0, 2 * quarter(w)))
         local[w].wait()
 
-    others = ((ACROSS, across), (RIGHT, right), (LEFT, left))
+    others = ((RIGHT, right), (LEFT, left), (ACROSS, across))
 
     def gather_start(name, src, s):
         dst = gathered[name].at[rows_of(s), part(t)]

time: 119 us -> 119 us (level)
  no operation moved by 1% of the time
where the time goes in v3:
time: 119 us; the launch traced here: 118 us
  Pallas kernels  117 us (98%)
    pallas_call x1, Pallas kernels, on_device(): pl.pallas_call(kernel, out_shape=(out((TOK, CH), bf16), out((TOK, CH), f3...  114 us
    pallas_call x1, Pallas kernels, on_device(): pl.pallas_call(deliver_kernel, out_shape=(*(out(a.shape, a.dtype) for a i...  3.52 us

profile of v3, /device:TPU:0, one launch (start us, length us, event | category | flops | bytes accessed | tf_op | source)
XLA Modules:
  0.0 118.2 jit_solution(4253043537034119834)
XLA Ops:
  0.6 113.8 %shard_map.177 = (bf16[512,256]{1,0:T(8,128)(2,1)}, f32[512,256]{1,0:T(8,128)}, f32[3,32,256]{2,1,0:T(8,128)}, f32[32,256]{1,0:T(8,128)}, f32[32,1152]{1,0:T(8,1...) custom-call(bf16[512,256]{1,0:T(8,128)(2,1)} %bitcast.11, bf16[512,256]{1,0:T(8,128)(2,1)} %bitcast.12, ...), custom_call_target="tpu_custom_call" | custom-call | tf_op jit(solution)/shard_map/pallas_call | solution.py:690
  114.5 3.5 %shard_map.178 = (bf16[512,256]{1,0:T(8,128)(2,1)}, f32[512,256]{1,0:T(8,128)}, f32[3,32,256]{2,1,0:T(8,128)}, f32[32,256]{1,0:T(8,128)}, f32[32,1152]{1,0:T(8,1...) custom-call(f32[8,256]{1,0:T(8,128)} %get-tuple-element.28.refs_0_, ...), custom_call_target="tpu_custom_call" | custom-call | tf_op jit(solution)/shard_map/pallas_call | solution.py:720

commit v4 on v3

--- a/solution.py
+++ b/solution.py
@@ -16,6 +16,7 @@
 RIGHT, LEFT, ACROSS, CORE, Z1, X1, Z3, X3, NEXT, PREV, X2, Z2, Z1C, Z2C, Z3C = range(15)
 AHEAD, GATHER, SUM, TOTAL, GRAD, GAINS, EDGE, BACK, SMALL = range(9)
 X, COT, Q, B = range(20, 24)
+RING_GATHERS, RING_SUMS = (X, COT), ()
 def scratch():
     v = pltpu.VMEM
     shapes = dict(
@@ -41,6 +42,7 @@
         gated=v((TOK, CH), bf16),
         ys=v((4, 2, 3, SEQ, CH), bf16),
         yr=v((4, 2, 3, SEQ, CH), bf16),
+        yo=v((4, 2, 2, SEQ // 2, CH), bf16),
         own=v((4, TOK, CH), f32),
         resid=v((TOK, CH), f32),
         tg=v((SEQ, HID), f32),
@@ -62,8 +64,8 @@
         terms=[v((2, 2, 16, 16, n), bf16) for n in COLS],
         paired=[v((2, 16, 16, n), bf16) for n in COLS],
         came=[v((2, 15, 16, n), bf16) for n in COLS],
-        ssem=pltpu.SemaphoreType.DMA((24,)),
-        rsem=pltpu.SemaphoreType.DMA((64,)),
+        ssem=pltpu.SemaphoreType.DMA((28,)),
+        rsem=pltpu.SemaphoreType.DMA((65,)),
         lsem=pltpu.SemaphoreType.DMA((7,)),
     )
     return shapes
@@ -206,47 +208,72 @@
         arrived((AHEAD, w, 2), piece(w, 1 - shard, 0, 2 * quarter(w)))
         local[w].wait()
 
-    others = ((RIGHT, right), (LEFT, left), (ACROSS, across))
-
     def gather_start(name, src, s):
-        dst = gathered[name].at[rows_of(s), part(t)]
-        for where, _ in others:
-            send((GATHER, name, s), GATHER, src, dst, where)
+        half = SEQ // 2
+
+        def go(key, first, where, count=half):
+            dst = gathered[name].at[pl.ds(s * SEQ + first, count), part(t)]
+            send((GATHER, name, s, key), (GATHER, name), src.at[pl.ds(first, count)], dst, where)
+
+        if name not in RING_GATHERS:
+            for where in (RIGHT, LEFT, ACROSS):
+                go(ACROSS, 0, where, SEQ)
+            return
+        go(RIGHT, 0, RIGHT)
+        go(LEFT, half, LEFT)
+        go(ACROSS, half, RIGHT)
+        go(ACROSS, 0, LEFT)
+
+    def gather_relay(name, s):
+        if name not in RING_GATHERS:
+            return
+        half, whole = SEQ // 2, gathered[name]
+        a = whole.at[pl.ds(s * SEQ, half), part(left)]
+        arrived((GATHER, name, s, RIGHT), a)
+        send((GATHER, name, s, ACROSS), (GATHER, name), a, a, RIGHT)
+        b = whole.at[pl.ds(s * SEQ + half, half), part(right)]
+        arrived((GATHER, name, s, LEFT), b)
+        send((GATHER, name, s, ACROSS), (GATHER, name), b, b, LEFT)
 
     def gather_finish(name, s):
-        arrived((GATHER, name, s), r.ys.at[0, 0])
-
-    def ring_start(name, src, s):
-        dst = gathered[name].at[rows_of(s), part(t)]
-        send((GATHER, name, s, RIGHT), name, src, dst, RIGHT)
-        send((GATHER, name, s, LEFT), name, src, dst, LEFT)
-
-    def ring_relay(name, s):
-        whole = gathered[name]
-        arrived((GATHER, name, s, RIGHT), whole.at[rows_of(s), part(left)])
-        a = whole.at[pl.ds(s * SEQ, SEQ // 2), part(left)]
-        send((GATHER, name, s, X1), name, a, a, RIGHT)
-        arrived((GATHER, name, s, LEFT), whole.at[rows_of(s), part(right)])
-        b = whole.at[pl.ds(s * SEQ + SEQ // 2, SEQ // 2), part(right)]
-        send((GATHER, name, s, X3), name, b, b, LEFT)
-
-    def ring_finish(name, s):
-        whole = gathered[name]
-        arrived((GATHER, name, s, X1), whole.at[pl.ds(s * SEQ, SEQ // 2), part(across)])
-        arrived((GATHER, name, s, X3), whole.at[pl.ds(s * SEQ + SEQ // 2, SEQ // 2), part(across)])
+        arrived((GATHER, name, s, ACROSS), r.ys.at[0, 0, pl.ds(0, 2 if name in RING_GATHERS else 3)])
+
+    top, low = pl.ds(0, SEQ // 2), pl.ds(SEQ // 2, SEQ // 2)
 
     def sum_start(ph, s, block):
-        for slot, (where, n) in enumerate(others):
-            r.ys[ph, s, slot] = block(n).astype(bf16)
-            send((SUM, ph, s), SUM, r.ys.at[ph, s, slot], r.yr.at[ph, s, slot], where)
+        ys, yr, yo = r.ys.at[ph, s], r.yr.at[ph, s], r.yo.at[ph, s]
+        if ph not in RING_SUMS:
+            for slot, (where, n) in enumerate(((RIGHT, right), (LEFT, left), (ACROSS, across))):
+                ys[slot] = block(n).astype(bf16)
+                send((SUM, ph, s, ACROSS), (SUM, ph), ys.at[slot], yr.at[slot], where)
+            r.own[ph, rows_of(s), :] = block(t)
+            return
+        ys[2] = block(across).astype(bf16)
+        send((SUM, ph, s, RIGHT), (SUM, ph), ys.at[2, top], yo.at[0], RIGHT)
+        send((SUM, ph, s, LEFT), (SUM, ph), ys.at[2, low], yo.at[1], LEFT)
+        ys[0] = block(right).astype(bf16)
+        send((SUM, ph, s, ACROSS), (SUM, ph), ys.at[0, low], yr.at[0, low], RIGHT)
+        ys[1] = block(left).astype(bf16)
+        send((SUM, ph, s, ACROSS), (SUM, ph), ys.at[1, top], yr.at[1, top], LEFT)
         r.own[ph, rows_of(s), :] = block(t)
 
+    def sum_relay(ph, s):
+        if ph not in RING_SUMS:
+            return
+        ys, yr, yo = r.ys.at[ph, s], r.yr.at[ph, s], r.yo.at[ph, s]
+        arrived((SUM, ph, s, RIGHT), yo.at[0])
+        ys[0, top, :] = (ys[0, top, :].astype(f32) + yo[0].astype(f32)).astype(bf16)
+        send((SUM, ph, s, ACROSS), (SUM, ph), ys.at[0, top], yr.at[0, top], RIGHT)
+        arrived((SUM, ph, s, LEFT), yo.at[1])
+        ys[1, low, :] = (ys[1, low, :].astype(f32) + yo[1].astype(f32)).astype(bf16)
+        send((SUM, ph, s, ACROSS), (SUM, ph), ys.at[1, low], yr.at[1, low], LEFT)
+
     def sum_finish(ph, s):
-        arrived((SUM, ph, s), r.yr.at[ph, s])
+        arrived((SUM, ph, s, ACROSS), r.yr.at[ph, s, pl.ds(0, 2 if ph in RING_SUMS else 3)])
 
     def summed(ph, s, i, n):
         total = r.own[ph, pl.ds(s * SEQ + i, n), :]
-        for slot in range(3):
+        for slot in range(2 if ph in RING_SUMS else 3):
             total = total + r.yr[ph, s, slot, pl.ds(i, n), :].astype(f32)
         return total
 
@@ -366,7 +393,9 @@
     for w in (OUT, GATE, UP, DOWN):
         weight_cross(w)
     for s in range(2):
-        ring_start(COT, cot_hbm.at[rows_of(s)], s)
+        gather_relay(X, s)
+    for s in range(2):
+        gather_start(COT, cot_hbm.at[rows_of(s)], s)
     weight_around(IN)
 
     def normalise(s):
@@ -398,6 +427,8 @@
     normalise(1)
     project(1)
     weight_share(OUT)
+    gather_relay(COT, 0)
+    gather_relay(COT, 1)
     weight_around(GATE)
 
     def branch(s):
@@ -420,10 +451,10 @@
     weight_ready(OUT)
     branch(0)
     branch(1)
-    ring_relay(COT, 0)
-    ring_relay(COT, 1)
     weight_around(UP)
     weight_share(GATE)
+    sum_relay(0, 0)
+    sum_relay(0, 1)
 
     def second(s):
         sum_finish(0, s)
@@ -441,6 +472,8 @@
     weight_around(DOWN)
     weight_share(UP)
     local[COT].wait()
+    gather_relay(Q, 0)
+    gather_relay(Q, 1)
 
     def feed(s):
         gather_finish(Q, s)
@@ -461,12 +494,14 @@
             weight_ready(UP)
         for cols in slices:
             r.tu[:, cols] = nn(q, r.wu[:, cols])
-        ring_finish(COT, s)
+        gather_finish(COT, s)
         if s == 0:
             weight_ready(DOWN)
         c = r.cg[rows_of(s), :]
         for cols in slices:
             r.td[:, cols] = nt(c, r.wd[cols, :])
+        if s == 1:
+            sum_relay(1, 0)
 
         def body(i, rows):
             here = pl.ds(i, 16)
@@ -522,6 +557,8 @@
 
     through_norm(0)
     grad_product(GATE, r.qg, r.eg)
+    sum_relay(1, 1)
+    gather_relay(B, 0)
     grad_product(UP, r.qg, r.eu)
     through_norm(1)
 
@@ -577,16 +614,20 @@
         totals_start(1, s, r.lanes[...])
 
     back(0)
+    gather_relay(B, 1)
     grad_product(DOWN, r.cg, r.hid)
     grad_first(UP)
     mixer(0)
+    sum_relay(2, 0)
     back(1)
     grad_product(OUT, r.bg, r.gated)
+    sum_relay(3, 0)
     grad_second(GATE)
     grad_first(DOWN)
     mixer(1)
     grad_product(IN, r.n1, r.dproj)
     deliver(1)
+    sum_relay(3, 1)
     grad_second(UP)
     grad_first(OUT)
 
@@ -609,6 +650,7 @@
     finish(0)
     grad_first(IN)
     grad_second(DOWN)
+    sum_relay(2, 1)
     grad_last(GATE)
     finish(1)
     for n, where in enumerate((CORE, Z1, Z2, Z3, Z1C, Z2C, Z3C)):
@@ -638,9 +680,11 @@
     g_small[...] = total
     grad_last(IN)
 
-    left_all(SUM, r.ys)
-    left_all(GATHER, r.ys.at[pl.ds(0, 3)])
-    left_all(COT, r.ys.at[0])
+    assert len(came_ids) <= rsem.shape[0] and len(sent_ids) <= ssem.shape[0]
+    for ph in range(4):
+        left_all((SUM, ph), r.ys.at[ph])
+    for name in gathered:
+        left_all((GATHER, name), r.ys.at[0])
     left_all(TOTAL, r.rsr)
     left_all(GAINS, r.rsr.at[0, 0])
     left_all(SMALL, r.sumr)

time: 119 us -> 117 us (0.983)
    pallas_call x1, Pallas kernels: 114 us -> 112 us  [on_device(): pl.pallas_call(kernel, out_shape=(out((TOK, CH), bf16), out((TOK, CH), f3...]
where the time goes in v4:
time: 117 us
  Pallas kernels  116 us (99%)
    pallas_call x1, Pallas kernels, on_device(): pl.pallas_call(kernel, out_shape=(out((TOK, CH), bf16), out((TOK, CH), f3...  112 us
    pallas_call x1, Pallas kernels, on_device(): pl.pallas_call(deliver_kernel, out_shape=(*(out(a.shape, a.dtype) for a i...  3.52 us

profile of v4, /device:TPU:0, one launch (start us, length us, event | category | flops | bytes accessed | tf_op | source)
XLA Modules:
  0.0 116.8 jit_solution(17512457797993563121)
XLA Ops:
  0.6 112.5 %shard_map.177 = (bf16[512,256]{1,0:T(8,128)(2,1)}, f32[512,256]{1,0:T(8,128)}, f32[3,32,256]{2,1,0:T(8,128)}, f32[32,256]{1,0:T(8,128)}, f32[32,1152]{1,0:T(8,1...) custom-call(bf16[512,256]{1,0:T(8,128)(2,1)} %bitcast.11, bf16[512,256]{1,0:T(8,128)(2,1)} %bitcast.12, ...), custom_call_target="tpu_custom_call" | custom-call | tf_op jit(solution)/shard_map/pallas_call | solution.py:734
  113.1 3.5 %shard_map.178 = (bf16[512,256]{1,0:T(8,128)(2,1)}, f32[512,256]{1,0:T(8,128)}, f32[3,32,256]{2,1,0:T(8,128)}, f32[32,256]{1,0:T(8,128)}, f32[32,1152]{1,0:T(8,1...) custom-call(f32[8,256]{1,0:T(8,128)} %get-tuple-element.28.refs_0_, ...), custom_call_target="tpu_custom_call" | custom-call | tf_op jit(solution)/shard_map/pallas_call | solution.py:764
